TPU v7x, 256 devices: a whole 4x4x8 slice. The times are simulated.
256 devices in a mesh: ctx: 16 (over x, y), head: 4 (over z_hi), dp: 4 (over z_lo, core).
Axes of the slice: x: 4, y: 4, z: 8 (z_hi: 4, z_lo: 2; z = z_hi * 2 + z_lo), core: 2. Of those that a mesh axis runs over, the one named last changes fastest.
Arguments:
- query_nope: bfloat16 [4, 2048, 4096], P('dp', 'ctx', 'head'), may hold values from -6 to 6
- query_rope: bfloat16 [4, 2048, 2048], P('dp', 'ctx', 'head'), may hold values from -8 to 8
- latent: bfloat16 [4, 2048, 512], P('dp', 'ctx'), may hold values from -6 to 6
- rope_key: bfloat16 [4, 2048, 64], P('dp', 'ctx'), may hold values from -8 to 8
- key_up: bfloat16 [512, 4096], P(None, 'head'), may hold values from -0.25 to 0.25
- value_up: bfloat16 [512, 4096], P(None, 'head'), may hold values from -0.25 to 0.25
- grad_out: bfloat16 [4, 2048, 4096], P('dp', 'ctx', 'head'), may hold values from -6 to 6
- group_order: int32 [32], replicated, may hold values from 0 to 31, each once
Outputs:
- latent_grad: bfloat16 [4, 2048, 512], P('dp', 'ctx', 'head')
- key_up_grad: float32 [512, 4096], P(None, 'head')
- value_up_grad: float32 [512, 4096], P(None, 'head')
Inputs may be any that keep to these rules, and one draw needn't show every extreme that they name: `group_order`: a permutation of the 32 group numbers.
All inputs are finite; a program needn't handle non-finite values.
Results may differ from a plain program's by a relative error of at most 0.0091.
Values may be sent and summed in bfloat16 or wider, within the bound.
A program may use at most 64 MiB of HBM per device.

v0:
```python
import math

import jax
import jax.numpy as jnp
from jax import lax
from jax.sharding import PartitionSpec as P

HEAD_DIM = 128


def contract(left_side, right_side, left_dim, right_dim):
    return lax.dot_general(
        left_side,
        right_side,
        (((left_dim,), (right_dim,)), ((), ())),
        preferred_element_type=jnp.float32,
    )


def positions(group_order, row_count, block_rows):
    row_ids = jnp.arange(row_count, dtype=jnp.int32)
    blocks = row_ids // block_rows
    onehot = blocks[:, None] == jnp.arange(group_order.shape[0], dtype=jnp.int32)[None, :]
    starts = jnp.sum(jnp.where(onehot, group_order[None, :], 0), axis=1)
    return starts * block_rows + row_ids % block_rows


def head_backward(
    query_nope, query_rope, grad_out, key_up, value_up, latent, rope_key, visible, factor
):
    query_lat = contract(query_nope, key_up, 1, 1).astype(jnp.bfloat16)
    scores = (contract(query_lat, latent, 1, 1) + contract(query_rope, rope_key, 1, 1)) * factor
    scores = jnp.where(visible, scores, -jnp.inf)
    largest = jnp.max(scores, axis=1, keepdims=True)
    lifted = jnp.exp(scores - largest)
    totals = jnp.sum(lifted, axis=1, keepdims=True)
    attn_probs = lifted / totals
    probs_low = attn_probs.astype(jnp.bfloat16)
    out_lat = contract(probs_low, latent, 1, 0)
    out_low = out_lat.astype(jnp.bfloat16)
    grad_lat = contract(grad_out, value_up, 1, 1)
    grad_low = grad_lat.astype(jnp.bfloat16)
    row_dot = jnp.sum(grad_lat * out_lat, axis=1, keepdims=True)
    grad_probs = contract(grad_low, latent, 1, 1)
    grad_scores = (attn_probs * (grad_probs - row_dot) * factor).astype(jnp.bfloat16)
    grad_query = contract(grad_scores, latent, 1, 0).astype(jnp.bfloat16)
    latent_part = contract(probs_low, grad_low, 0, 0) + contract(grad_scores, query_lat, 0, 0)
    key_part = contract(grad_query, query_nope, 0, 0)
    value_part = contract(out_low, grad_out, 0, 0)
    return (latent_part, key_part, value_part)


def shards(query_nope, query_rope, latent, rope_key, key_up, value_up, grad_out, group_order):
    local_rows = query_nope.shape[1]
    head_count = key_up.shape[1] // HEAD_DIM
    rope_width = rope_key.shape[2]
    latent_width = latent.shape[2]
    factor = 1.0 / math.sqrt(HEAD_DIM + rope_width)
    all_latent, all_rope = (
        lax.all_gather(latent, "ctx", axis=1, tiled=True),
        lax.all_gather(rope_key, "ctx", axis=1, tiled=True),
    )
    key_rows = all_latent.shape[1]
    key_place = positions(group_order, key_rows, local_rows // 2)
    offset_rows = lax.axis_index("ctx") * local_rows
    own_place = lax.dynamic_slice_in_dim(key_place, offset_rows, local_rows)
    visible = key_place[None, :] <= own_place[:, None]
    key_heads = key_up.reshape(latent_width, head_count, HEAD_DIM).transpose(1, 0, 2)
    value_heads = value_up.reshape(latent_width, head_count, HEAD_DIM).transpose(1, 0, 2)

    def one_sequence(members):
        nope_seq, rope_seq, latent_seq, rkey_seq, grad_seq = members
        nope_heads = nope_seq.reshape(local_rows, head_count, HEAD_DIM).transpose(1, 0, 2)
        rope_heads = rope_seq.reshape(local_rows, head_count, rope_width).transpose(1, 0, 2)
        grad_heads = grad_seq.reshape(local_rows, head_count, HEAD_DIM).transpose(1, 0, 2)

        def one_head(running, head_items):
            nope_h, rope_h, grad_h, key_h, value_h = head_items
            latent_part, key_part, value_part = head_backward(
                nope_h, rope_h, grad_h, key_h, value_h, latent_seq, rkey_seq, visible, factor
            )
            return (running + latent_part, (key_part, value_part))

        zero_sum = jnp.zeros((key_rows, latent_width), jnp.float32)
        latent_sum, parts = lax.scan(
            one_head, zero_sum, (nope_heads, rope_heads, grad_heads, key_heads, value_heads)
        )
        return (latent_sum, parts[0], parts[1])

    totals, key_parts, value_parts = lax.map(
        one_sequence, (query_nope, query_rope, all_latent, all_rope, grad_out)
    )
    owned_rows = lax.psum_scatter(totals, "ctx", scatter_dimension=1, tiled=True)
    latent_share = lax.psum_scatter(owned_rows, "head", scatter_dimension=2, tiled=True)
    key_local = (
        jnp.sum(key_parts, axis=0).transpose(1, 0, 2).reshape(latent_width, head_count * HEAD_DIM)
    )
    value_local = (
        jnp.sum(value_parts, axis=0).transpose(1, 0, 2).reshape(latent_width, head_count * HEAD_DIM)
    )
    key_up_grad, value_up_grad = lax.psum((key_local, value_local), ("ctx", "dp"))
    return (latent_share.astype(jnp.bfloat16), key_up_grad, value_up_grad)


def solution(mesh):
    in_specs = (
        P("dp", "ctx", "head"),
        P("dp", "ctx", "head"),
        P("dp", "ctx", None),
        P("dp", "ctx", None),
        P(None, "head"),
        P(None, "head"),
        P("dp", "ctx", "head"),
        P(),
    )
    out_specs = (P("dp", "ctx", "head"), P(None, "head"), P(None, "head"))
    return jax.shard_map(shards, mesh=mesh, in_specs=in_specs, out_specs=out_specs, check_vma=False)
```

profile of v0, /device:TPU:1, one launch (start us, length us, event | category | flops | bytes accessed | tf_op | source)
XLA Modules:
  0.0 897.2 jit_solution(18234866859840560525)
XLA Ops:
  9.9 1.8 copy.27
  11.7 1.8 copy.31
  15.6 22.9 %all_gather.7 = bf16[1,2048,64]{2,1,0:T(8,128)(2,1)} all-gather(bf16[1,128,64]{2,1,0:T(8,128)(2,1)S(1)} %copy.30), channel_id=1, replica_groups=mesh['ctx'=16,'head'=4,'dp'=4] {'ctx'}, dimensions={1}, use_global_device_ids=true | all-gather | bytes 278528 | tf_op jit(solution)/shard_map/all_gather | solution.py:61
  38.5 25.0 %all-gather.2.cloned.1.call-done = bf16[1,2048,512]{2,1,0:T(8,128)(2,1)} async-done(((bf16[1,128,512]{2,1,0:T(8,128)(2,1)}), bf16[1,2048,512]{2,1,0:T(8,128)(2,1)}) %all-gather.2.cloned.1.call-update) | async-done | bytes 2097168 | tf_op jit(solution)/shard_map/all_gather | solution.py:60
  63.5 146.4 %while.26 = (s32[]{:T(128)}, f32[2048,512]{1,0:T(8,128)}, f32[8,512,128]{2,1,0:T(8,128)}, f32[8,512,128]{2,1,0:T(8,128)}, bf16[8,128,128]{1,2,0:T(8,128)(2,1)}, ...) while((s32[]{:T(128)}, f32[2048,512]{1,0:T(8,128)}, ...), condition=%wide.region_5.6_spmd.clone, body=%wide.region_1.5_spmd.clone.sunk | while | flops 1719795328 | bytes 90610088 | solution.py:85
  64.6 2.4 fusion.107
  70.3 1.7 fusion.112
  72.0 1.7 fusion.114
  73.7 2.4 fusion.113
  79.8 1.9 copy-done.2
  82.9 2.4 fusion.107
  88.6 1.7 fusion.112
  90.3 1.7 fusion.114
  92.0 2.4 fusion.113
  98.2 1.9 copy-done.2
  101.2 2.4 fusion.107
  107.0 1.7 fusion.112
  108.6 1.7 fusion.114
  110.3 2.4 fusion.113
  116.5 1.9 copy-done.2
  119.5 2.4 fusion.107
  125.3 1.7 fusion.112
  126.9 1.7 fusion.114
  128.6 2.4 fusion.113
  134.8 1.9 copy-done.2
  137.8 2.4 fusion.107
  143.6 1.7 fusion.112
  145.2 1.7 fusion.114
  146.9 2.4 fusion.113
  153.1 1.9 copy-done.2
  156.1 2.4 fusion.107
  161.9 1.7 fusion.112
  163.5 1.7 fusion.114
  165.2 2.4 fusion.113
  171.4 1.9 copy-done.2
  174.4 2.4 fusion.107
  181.8 1.7 fusion.114
  183.5 2.4 fusion.113
  189.7 1.9 copy-done.2
  192.7 2.4 fusion.107
  200.2 1.7 fusion.114
  201.8 2.4 fusion.113
  208.0 1.9 copy-done.2
  210.0 81.4 %reduce-scatter.3.cloned.1.call-done = f32[1,128,512]{2,1,0:T(8,128)} async-done(((f32[1,2048,512]{2,1,0:T(8,128)}), f32[1,128,512]{2,1,0:T(8,128)}) %reduce-scatter.3.cloned.1.call-update) | async-done | bytes 262160 | tf_op jit(solution)/shard_map/reduce_scatter | solution.py:93
  291.5 4.2 copy_bitcast_fusion
  295.7 22.9 %reduce-scatter.5.cloned.1.call-done = f32[1,128,128]{2,1,0:T(8,128)} async-done(((f32[1,128,512]{2,1,0:T(8,128)}), f32[1,128,128]{2,1,0:T(8,128)}) %reduce-scatter.5.cloned.1.call-update) | async-done | bytes 65552 | tf_op jit(solution)/shard_map/reduce_scatter | solution.py:94
  320.0 566.0 %all-reduce.3.cloned.1.call-done = (f32[512,1024]{1,0:T(8,128)}, f32[512,1024]{1,0:T(8,128)}) async-done(((f32[512,1024]{1,0:T(8,128)}, f32[512,1024]{1,0:T(8,128)}), (f32[512,1024]{1,0:T(8,128)}, f32[512,1024]{1,0:T(8,128)})) %all-reduce.3.cloned.1.call-update) | async-done | bytes 4194320 | tf_op jit(solution)/shard_map/psum | solution.py:101
  886.0 3.3 copy.65
  (225 shorter events, 75.7 us)
Async XLA Ops:
  7.2 6.3 copy-start.9
  7.2 6.8 copy-start.10
  7.2 56.3 %all-gather.2.cloned.1.call-start = ((), (), s32[]{:S(2)}) async-start(), calls=%async_computation.2 | async-start | bytes 2228224 | tf_op jit(solution)/shard_map/all_gather | solution.py:60
  7.9 283.5 %reduce-scatter.3.cloned.1.call-start = ((), (), s32[]{:S(2)}) async-start(), calls=%async_computation.3 | async-start | bytes 4456448 | tf_op jit(solution)/shard_map/reduce_scatter | solution.py:93
  63.5 4.0 copy-start.11
  63.5 3.5 copy-start.4
  76.1 2.3 copy-start.3
  78.4 3.4 copy-start.6
  78.4 3.4 copy-start.12
  81.8 4.0 copy-start.11
  81.8 3.5 copy-start.4
  94.4 2.3 copy-start.3
  96.7 3.4 copy-start.6
  96.7 3.4 copy-start.12
  100.1 4.0 copy-start.11
  100.1 3.5 copy-start.4
  112.7 2.3 copy-start.3
  115.0 3.4 copy-start.6
  115.0 3.4 copy-start.12
  118.4 4.0 copy-start.11
  118.4 3.5 copy-start.4
  131.0 2.3 copy-start.3
  133.3 3.4 copy-start.6
  133.3 3.4 copy-start.12
  136.7 4.0 copy-start.11
  136.7 3.5 copy-start.4
  149.3 2.3 copy-start.3
  151.6 3.4 copy-start.6
  151.6 3.4 copy-start.12
  155.0 4.0 copy-start.11
  155.0 3.5 copy-start.4
  167.6 2.3 copy-start.3
  169.9 3.4 copy-start.6
  169.9 3.4 copy-start.12
  173.3 4.0 copy-start.11
  173.3 3.5 copy-start.4
  186.0 2.3 copy-start.3
  188.3 3.4 copy-start.6
  188.3 3.4 copy-start.12
  191.6 4.0 copy-start.11
  191.6 3.5 copy-start.4
  204.3 2.3 copy-start.3
  206.6 3.4 copy-start.6
  206.6 3.4 copy-start.12
  209.9 81.5 %copy-start.8 = (f32[8,512,128]{2,1,0:T(8,128)S(1)}, f32[8,512,128]{2,1,0:T(8,128)}, u32[]{:S(2)}) copy-start(f32[8,512,128]{2,1,0:T(8,128)} %get-tuple-element.104) | copy-start | bytes 6291460
  210.0 108.6 %reduce-scatter.5.cloned.1.call-start = ((), (), s32[]{:S(2)}) async-start(), calls=%async_computation.4 | async-start | bytes 327680 | tf_op jit(solution)/shard_map/reduce_scatter | solution.py:94
  291.4 594.6 %all-reduce.3.cloned.1.call-start = ((), (), s32[]{:S(2)}) async-start(), calls=%async_computation.5 | async-start | bytes 8388608 | tf_op jit(solution)/shard_map/psum | solution.py:101
  886.0 3.3 copy-start.7
  (33 other events, 56.6 us)
Sparse Core Ops, SparseCore 0:
  10.5 53.0 all-gather.1
  210.1 81.2 reduce-scatter.2
  294.1 24.4 reduce-scatter.4
  321.7 564.3 all-reduce.2
where the time goes:
time: 899 us; the launch traced here: 897 us
  waiting for transfers between devices  696 us (77%)
  matrix products  109 us (12%)
  local copies, waits for them, and re-layouts  50.2 us (6%)
  blocking collectives  22.9 us (3%)
  between operations  13.9 us (2%)
    psum x1, waiting for transfers between devices, shards(): lax.psum((key_local, value_local), ('ctx', 'dp'))  566 us
    dot_general x80, matrix products, contract(): lax.dot_general(left_side, right_side, (((left_dim,), (right_dim,)), ((),...  109 us
    reduce_scatter x1, waiting for transfers between devices, shards(): lax.psum_scatter(totals, 'ctx', scatter_dimension=1, tiled=True)  81.4 us
    while x144, local copies, waits for them, and re-layouts  34 us
    all_gather x1, waiting for transfers between devices, shards(): lax.all_gather(latent, 'ctx', axis=1, tiled=True)  25 us
    all_gather x1, blocking collectives, shards(): lax.all_gather(rope_key, 'ctx', axis=1, tiled=True)  22.9 us
    reduce_scatter x1, waiting for transfers between devices, shards(): lax.psum_scatter(owned_rows, 'head', scatter_dimension=2, tiled=True)  22.9 us
  transfers between devices with their start and end apart: 4, of which 4 were waited for; matrix products, arithmetic and copies ran while one was open for 1% of the time, Pallas kernels for 0%

commit v1 on v0

v1 whole, which is shorter than its diff:
```python
import functools
import math

import jax
import jax.numpy as jnp
from jax import lax
from jax.experimental import pallas as pl
from jax.experimental.pallas import tpu as pltpu
from jax.sharding import PartitionSpec as P

HEAD_DIM = 128
GROUP = 64
F32 = jnp.float32
BF16 = jnp.bfloat16
MESH = pl.DeviceIdType.MESH


def dot_nn(left, right):
    return lax.dot_general(left, right, (((1,), (0,)), ((), ())), preferred_element_type=F32)


def dot_nt(left, right):
    return lax.dot_general(left, right, (((1,), (1,)), ((), ())), preferred_element_type=F32)


def mult(value, factor):
    return pl.multiple_of(value * factor, factor)


def kernel(dims, *refs):
    (nx, ny, nh, nz, heads, latent, rope, factor) = dims
    (
        group_ref, lat_ref, rk_ref, qn_ref, qr_ref, ku_ref, vu_ref, go_ref,
        lat_out, key_out, val_out,
        kbuf, lat_t, qn, qr, ku, vu, go, rk,
        q_t, g_t, g_low, score, gprob, prob, dscore,
        bias, peak, total, inv, rdot,
        o_low, gq_low, g_nat, q_nat,
        lsend, l1a, l1b, l2as, l2bs, l2a, l2b, lzs, lzr, lat_v,
        w_own, w_core, w_acc, w1, w1s, w2, w2s, wz, w_out,
        in_sem, out_sem, ag_s, ag_r, l_s, l_r, l2_s, l2_r, lz_s, lz_r,
        wc_s, wc_r, w1_s, w1_r, w2_s, w2_r, wz_s, wz_r,
        vz_s, vz_r, v2_s, v2_r, v1_s, v1_r, vc_s, vc_r,
    ) = refs
    rows = 128
    blocks = nx * ny
    keys = blocks * rows
    cols = heads * HEAD_DIM
    wide = latent + 128
    chunk = ny * rows
    half_lat = latent // 2

    ctx = lax.axis_index("ctx")
    head = lax.axis_index("head")
    dp = lax.axis_index("dp")
    x, y = ctx // ny, lax.rem(ctx, ny)
    zl, core = dp // 2, lax.rem(dp, 2)

    def xs(off):
        return lax.rem(x + off, nx)

    def ys(off):
        return lax.rem(y + off, ny)

    def at_x(off):
        return {"ctx": xs(off) * ny + y}

    def at_y(off):
        return {"ctx": x * ny + ys(off)}

    def at_core():
        return {"dp": zl * 2 + 1 - core}

    def at_z(off):
        return {"dp": lax.rem(zl + off, nz) * 2 + core}

    def at_head(off):
        return {"head": lax.rem(head + off, nh)}

    x_offs = [o for o in (1, nx - 1, 2) if 0 < o < nx]
    x_offs = list(dict.fromkeys(x_offs))
    y_offs = list(dict.fromkeys([o for o in (1, ny - 1, 2) if 0 < o < ny]))
    partners = (
        [at_x(o) for o in x_offs] + [at_y(o) for o in y_offs] + [at_core()]
        + [at_z(o) for o in range(1, nz)] + [at_head(o) for o in range(1, nh)]
    )

    sends = []

    def send(src, dst, ssem, rsem, where):
        copy = pltpu.make_async_remote_copy(
            src_ref=src, dst_ref=dst, send_sem=ssem, recv_sem=rsem,
            device_id=where, device_id_type=MESH,
        )
        copy.start()
        sends.append(copy)

    def arrived(dst, ssem, rsem, where):
        pltpu.make_async_remote_copy(
            src_ref=dst, dst_ref=dst, send_sem=ssem, recv_sem=rsem,
            device_id=where, device_id_type=MESH,
        ).wait_recv()

    barrier = pltpu.get_barrier_semaphore()
    for where in partners:
        pl.semaphore_signal(barrier, inc=1, device_id=where, device_id_type=MESH)

    own_rows = pl.ds(mult(ctx, rows), rows)
    loads = [
        pltpu.make_async_copy(lat_ref, kbuf.at[own_rows, pl.ds(0, latent)], in_sem.at[0]),
        pltpu.make_async_copy(rk_ref, rk, in_sem.at[1]),
        pltpu.make_async_copy(qn_ref, qn, in_sem.at[2]),
        pltpu.make_async_copy(ku_ref, ku, in_sem.at[3]),
        pltpu.make_async_copy(qr_ref, qr, in_sem.at[4]),
        pltpu.make_async_copy(go_ref, go, in_sem.at[5]),
        pltpu.make_async_copy(vu_ref, vu, in_sem.at[6]),
    ]
    for copy in loads:
        copy.start()

    loads[1].wait()
    spread = lax.broadcasted_iota(jnp.int32, (rope, 128), 0)
    lane = lax.broadcasted_iota(jnp.int32, (rope, 128), 1)
    twice = jnp.where(spread == lax.rem(lane, rope), 1.0, 0.0).astype(BF16)
    kbuf[own_rows, pl.ds(latent, 128)] = dot_nn(rk[...], twice).astype(BF16)
    loads[0].wait()
    pl.semaphore_wait(barrier, len(partners))

    part = rows // 2

    def piece(block, half):
        return kbuf.at[pl.ds(pl.multiple_of(block * rows + half * part, part), part)]

    def gather_send(block, half, slot, where):
        send(piece(block, half), piece(block, half), ag_s.at[half, slot], ag_r.at[half, block], where)

    def gather_wait(block, half):
        arrived(piece(block, half), ag_s.at[half, 0], ag_r.at[half, block], at_x(1))

    slot = 0
    for k in range(max(len(x_offs), len(y_offs))):
        gather_send(ctx, 0, slot, at_x(x_offs[k]))
        gather_send(ctx, 1, slot, at_y(y_offs[k]))
        slot += 1
    for k in range(len(x_offs)):
        gather_send(ctx, 0, slot, at_y(y_offs[k]))
        gather_send(ctx, 1, slot, at_x(x_offs[k]))
        slot += 1

    for copy in loads[2:]:
        copy.wait()
    row_id = lax.broadcasted_iota(jnp.int32, (128, 128), 0)
    col_id = lax.broadcasted_iota(jnp.int32, (128, 128), 1)
    eye = row_id == col_id

    def head_cols(h):
        return pl.ds(mult(h, 128), 128)

    def project(h, carry):
        hc = head_cols(h)
        q_t[pl.ds(0, latent), hc] = dot_nt(ku[:, hc], qn[:, hc]).astype(BF16)
        pick = jnp.where(eye & (row_id // rope == lax.rem(h, 2)), 1.0, 0.0).astype(BF16)
        pair = qr[:, pl.ds(mult(h // 2, 128), 128)]
        q_t[pl.ds(latent, 128), hc] = dot_nt(pick, pair).astype(BF16)
        grad = dot_nt(vu[:, hc], go[:, hc])
        g_t[:, hc] = grad
        g_low[:, hc] = grad.astype(BF16)
        return carry

    lax.fori_loop(0, heads, project, 0)

    for k in range(len(x_offs)):
        block = xs(x_offs[k]) * ny + y
        gather_wait(block, 0)
        for o in y_offs:
            gather_send(block, 0, slot + k * len(y_offs) + y_offs.index(o), at_y(o))
        block = x * ny + ys(y_offs[k])
        gather_wait(block, 1)
        for o in x_offs:
            gather_send(block, 1, slot + k * len(x_offs) + x_offs.index(o), at_x(o))

    lanes = lax.broadcasted_iota(jnp.int32, (GROUP, 128), 1)
    downs = lax.broadcasted_iota(jnp.int32, (GROUP, 128), 0)
    own_low, own_high = group_ref[2 * ctx], group_ref[2 * ctx + 1]
    q_pos = jnp.where(lanes < GROUP, own_low * GROUP + lanes, own_high * GROUP + lanes - GROUP)
    peak[...] = jnp.full(peak.shape, -jnp.inf, F32)
    ident_r = lax.broadcasted_iota(jnp.int32, (latent, latent), 0)
    ident_c = lax.broadcasted_iota(jnp.int32, (latent, latent), 1)
    tile = 256
    tiles = cols // tile

    def tile_cols(n):
        return pl.ds(mult(n, tile), tile)

    for i in range(nx):
        xc = xs(([0] + x_offs)[i])
        for o in range(ny):
            block = xc * ny + ys(o)
            if o > 0:
                gather_wait(block, 0)
            if i > 0:
                gather_wait(block, 1)
        span = pl.ds(mult(xc, chunk), chunk)
        for b in range(ny):
            for g in range(2):
                k_pos = group_ref[2 * (xc * ny + b) + g] * GROUP + downs
                bias[pl.ds(b * rows + g * GROUP, GROUP), :] = jnp.where(k_pos <= q_pos, 0.0, -jnp.inf)

        def one_tile(n, carry, span=span):
            tc = tile_cols(n)
            s = dot_nn(kbuf[span, :], q_t[:, tc])
            mask = bias[...]
            s = s + jnp.concatenate([mask] * (tile // 128), axis=1)
            score[span, tc] = s
            peak[:, tc] = jnp.maximum(peak[:, tc], jnp.max(s, axis=0, keepdims=True))
            gprob[span, tc] = dot_nn(kbuf[span, pl.ds(0, latent)], g_low[:, tc])
            return carry

        lax.fori_loop(0, tiles, one_tile, 0)
        ident = jnp.where(ident_r == ident_c, 1.0, 0.0).astype(BF16)
        lat_t[:, span] = dot_nt(ident, kbuf[span, pl.ds(0, latent)]).astype(BF16)

    step = 256
    steps = keys // step
    total[...] = jnp.zeros(total.shape, F32)
    scale = factor * math.log2(math.e)

    def soften(i, carry):
        span = pl.ds(mult(i, step), step)
        p = jnp.exp2((score[span, :] - peak[...]) * scale)
        total[...] += jnp.sum(p, axis=0, keepdims=True)
        prob[span, :] = p.astype(BF16)
        return carry

    lax.fori_loop(0, steps, soften, 0)
    inv[...] = 1.0 / total[...]

    def read_out(n, carry):
        tc = tile_cols(n)
        o = dot_nn(lat_t[...], prob[:, tc]) * inv[:, tc]
        o_low[:, tc] = o.astype(BF16)
        rdot[:, tc] = jnp.sum(g_t[:, tc] * o, axis=0, keepdims=True)
        return carry

    lax.fori_loop(0, tiles, read_out, 0)

    core_rows = latent // 2
    hw = core_rows // 2

    def chain(w):
        first = ((nx, x, xs, at_x, x_offs), (ny, y, ys, at_y, y_offs))
        base = core * core_rows
        send(
            w_own.at[w, pl.ds(mult(1 - core, core_rows), core_rows)], w_core.at[w],
            wc_s.at[w], wc_r.at[w], at_core(),
        )
        yield
        arrived(w_core.at[w], wc_s.at[w], wc_r.at[w], at_core())
        mine = w_own[w, pl.ds(mult(core, core_rows), core_rows), :].astype(F32)
        w_acc[w] = (mine + w_core[w].astype(F32)).astype(BF16)
        for s in range(2):
            n1, i1, s1, a1, o1 = first[s]
            r = hw // n1
            for o in o1:
                send(
                    w_acc.at[w, pl.ds(pl.multiple_of(s * hw + s1(o) * r, r), r)], w1.at[w, s, o - 1],
                    w1_s.at[w, s, o - 1], w1_r.at[w, s, o - 1], a1(o),
                )
        yield
        for s in range(2):
            n1, i1, s1, a1, o1 = first[s]
            n2, i2, s2, a2, o2 = first[1 - s]
            r = hw // n1
            c = cols // n2
            acc = w_acc[w, pl.ds(pl.multiple_of(s * hw + i1 * r, r), r), :].astype(F32)
            for o in o1:
                arrived(w1.at[w, s, o - 1], w1_s.at[w, s, o - 1], w1_r.at[w, s, o - 1], a1(o))
                acc = acc + w1[w, s, o - 1].astype(F32)
            w1s[w, s] = acc
            for o in o2:
                send(
                    w1s.at[w, s, :, pl.ds(mult(s2(o), c), c)], w2.at[w, s, o - 1],
                    w2_s.at[w, s, o - 1], w2_r.at[w, s, o - 1], a2(o),
                )
        yield
        for s in range(2):
            n1, i1, s1, a1, o1 = first[s]
            n2, i2, s2, a2, o2 = first[1 - s]
            r = hw // n1
            c = cols // n2
            acc = w1s[w, s, :, pl.ds(mult(i2, c), c)]
            for o in o2:
                arrived(w2.at[w, s, o - 1], w2_s.at[w, s, o - 1], w2_r.at[w, s, o - 1], a2(o))
                acc = acc + w2[w, s, o - 1]
            w2s[w, s] = acc
            rz = r // nz
            for o in range(1, nz):
                send(
                    w2s.at[w, s, pl.ds(mult(lax.rem(zl + o, nz), rz), rz)], wz.at[w, s, o - 1],
                    wz_s.at[w, s, o - 1], wz_r.at[w, s, o - 1], at_z(o),
                )
        yield

        def place(s, i1, zi, i2, height, width):
            n1 = first[s][0]
            c = cols // first[1 - s][0]
            r = hw // n1
            top = pl.multiple_of(base + s * hw + i1 * r + zi * (r // nz), r // nz)
            return w_out.at[w, pl.ds(top, height), pl.ds(mult(i2, c), width)]

        for s in range(2):
            n1, i1, s1, a1, o1 = first[s]
            n2, i2, s2, a2, o2 = first[1 - s]
            r = hw // n1
            c = cols // n2
            rz = r // nz
            acc = w2s[w, s, pl.ds(mult(zl, rz), rz), :]
            for o in range(1, nz):
                arrived(wz.at[w, s, o - 1], wz_s.at[w, s, o - 1], wz_r.at[w, s, o - 1], at_z(o))
                acc = acc + wz[w, s, o - 1]
            spot = place(s, i1, zl, i2, rz, c)
            spot[...] = acc.astype(BF16)
            for o in range(1, nz):
                send(spot, spot, vz_s.at[w, s, o - 1], vz_r.at[w, s, o - 1], at_z(o))
        yield
        for s in range(2):
            n1, i1, s1, a1, o1 = first[s]
            n2, i2, s2, a2, o2 = first[1 - s]
            r = hw // n1
            c = cols // n2
            rz = r // nz
            for o in range(1, nz):
                spot = place(s, i1, lax.rem(zl + nz - o, nz), i2, rz, c)
                arrived(spot, vz_s.at[w, s, o - 1], vz_r.at[w, s, o - 1], at_z(o))
            spot = place(s, i1, 0, i2, r, c)
            for o in o2:
                send(spot, spot, v2_s.at[w, s, o - 1], v2_r.at[w, s, o - 1], a2(o))
        yield
        for s in range(2):
            n1, i1, s1, a1, o1 = first[s]
            n2, i2, s2, a2, o2 = first[1 - s]
            r = hw // n1
            c = cols // n2
            for o in o2:
                spot = place(s, i1, 0, s2(n2 - o), r, c)
                arrived(spot, v2_s.at[w, s, o - 1], v2_r.at[w, s, o - 1], a2(o))
            spot = place(s, i1, 0, 0, r, cols)
            for o in o1:
                send(spot, spot, v1_s.at[w, s, o - 1], v1_r.at[w, s, o - 1], a1(o))
        yield
        for s in range(2):
            n1, i1, s1, a1, o1 = first[s]
            r = hw // n1
            for o in o1:
                spot = place(s, s1(n1 - o), 0, 0, r, cols)
                arrived(spot, v1_s.at[w, s, o - 1], v1_r.at[w, s, o - 1], a1(o))
        spot = w_out.at[w, pl.ds(mult(core, core_rows), core_rows)]
        send(spot, spot, vc_s.at[w], vc_r.at[w], at_core())
        yield
        spot = w_out.at[w, pl.ds(mult(1 - core, core_rows), core_rows)]
        arrived(spot, vc_s.at[w], vc_r.at[w], at_core())
        out = pltpu.make_async_copy(w_out.at[w], (val_out, key_out)[w], out_sem.at[w])
        out.start()
        yield
        out.wait()
        yield

    def value_head(h, carry):
        hc = head_cols(h)
        w_own[0, :, hc] = dot_nn(o_low[:, hc], go[:, hc]).astype(BF16)
        return carry

    lax.fori_loop(0, heads, value_head, 0)
    value_chain, key_chain = chain(0), chain(1)
    next(value_chain)

    def rescale(h, carry):
        hc = head_cols(h)
        col = jnp.sum(jnp.where(eye, jnp.broadcast_to(inv[:, hc], (128, 128)), 0.0), axis=1, keepdims=True)
        g_nat[hc, :] = (dot_nt(go[:, hc], vu[:, hc]) * col).astype(BF16)
        q_nat[hc, :] = (dot_nt(qn[:, hc], ku[:, hc]) * (col * factor)).astype(BF16)
        return carry

    lax.fori_loop(0, heads, rescale, 0)

    def grade(i, carry):
        span = pl.ds(mult(i, step), step)
        ds = prob[span, :].astype(F32) * (gprob[span, :] - rdot[...])
        dscore[span, :] = ds.astype(BF16)
        return carry

    lax.fori_loop(0, steps, grade, 0)

    def query_grad(n, carry):
        tc = tile_cols(n)
        gq_low[:, tc] = (dot_nn(lat_t[...], dscore[:, tc]) * (inv[:, tc] * factor)).astype(BF16)
        return carry

    lax.fori_loop(0, tiles, query_grad, 0)

    def key_head(h, carry):
        hc = head_cols(h)
        w_own[1, :, hc] = dot_nn(gq_low[:, hc], qn[:, hc]).astype(BF16)
        return carry

    lax.fori_loop(0, heads, key_head, 0)
    next(key_chain)
    next(value_chain)

    order = x_offs[::-1] + [0]
    for i in range(nx):
        xo = order[i]
        xc = xs(xo)
        span = pl.ds(mult(xc, chunk), chunk)

        def latent_tile(n, carry, span=span):
            cs = pl.ds(mult(n, half_lat), half_lat)
            part_sum = dot_nn(prob[span, :], g_nat[:, cs]) + dot_nn(dscore[span, :], q_nat[:, cs])
            lsend[span, cs] = part_sum.astype(BF16)
            return carry

        lax.fori_loop(0, 2, latent_tile, 0)
        if xo > 0:
            send(
                lsend.at[span, pl.ds(0, half_lat)], l1a.at[xo - 1],
                l_s.at[0, xo - 1], l_r.at[0, xo - 1], at_x(xo),
            )
        for o in y_offs:
            block = pl.ds(mult(xc * ny + ys(o), rows), rows)
            send(
                lsend.at[block, pl.ds(half_lat, half_lat)], l1b.at[o - 1, xc],
                l_s.at[1 + xo, o - 1], l_r.at[1 + xo, o - 1], at_y(o),
            )
        next((key_chain, value_chain)[i % 2])

    for _ in range(2):
        next(key_chain)
        next(value_chain)

    span = pl.ds(mult(x, chunk), chunk)
    acc = lsend[span, pl.ds(0, half_lat)].astype(F32)
    for o in x_offs:
        arrived(l1a.at[o - 1], l_s.at[0, o - 1], l_r.at[0, o - 1], at_x(o))
        acc = acc + l1a[o - 1].astype(F32)
    l2as[...] = acc.astype(BF16)
    for o in y_offs:
        send(
            l2as.at[pl.ds(mult(ys(o), rows), rows)], l2a.at[o - 1],
            l2_s.at[0, o - 1], l2_r.at[0, o - 1], at_y(o),
        )
    for o in y_offs:
        for xo in range(nx):
            arrived(
                l1b.at[o - 1, xs(xo)], l_s.at[1 + xo, o - 1],
                l_r.at[1 + xo, o - 1], at_y(o),
            )
    for xc in range(nx):
        block = pl.ds(mult(xc * ny + y, rows), rows)
        acc = lsend[block, pl.ds(half_lat, half_lat)].astype(F32)
        for o in y_offs:
            acc = acc + l1b[o - 1, xc].astype(F32)
        l2bs[xc] = acc.astype(BF16)
    for o in x_offs:
        send(l2bs.at[xs(o)], l2b.at[o - 1], l2_s.at[1, o - 1], l2_r.at[1, o - 1], at_x(o))
    next(key_chain)
    next(value_chain)

    acc = l2as[pl.ds(mult(y, rows), rows), :].astype(F32)
    for o in y_offs:
        arrived(l2a.at[o - 1], l2_s.at[0, o - 1], l2_r.at[0, o - 1], at_y(o))
        acc = acc + l2a[o - 1].astype(F32)
    lzs[:, pl.ds(0, half_lat)] = acc.astype(BF16)
    acc = l2bs[x].astype(F32)
    for o in x_offs:
        arrived(l2b.at[o - 1], l2_s.at[1, o - 1], l2_r.at[1, o - 1], at_x(o))
        acc = acc + l2b[o - 1].astype(F32)
    lzs[:, pl.ds(half_lat, half_lat)] = acc.astype(BF16)
    share = latent // nh
    for o in range(1, nh):
        send(
            lzs.at[:, pl.ds(mult(lax.rem(head + o, nh), share), share)], lzr.at[o - 1],
            lz_s.at[o - 1], lz_r.at[o - 1], at_head(o),
        )
    next(key_chain)
    next(value_chain)
    acc = lzs[:, pl.ds(mult(head, share), share)].astype(F32)
    for o in range(1, nh):
        arrived(lzr.at[o - 1], lz_s.at[o - 1], lz_r.at[o - 1], at_head(o))
        acc = acc + lzr[o - 1].astype(F32)
    lat_v[...] = acc.astype(BF16)
    out = pltpu.make_async_copy(lat_v, lat_out, out_sem.at[2])
    out.start()
    live = [value_chain, key_chain]
    while live:
        for c in list(live):
            if next(c, "end") == "end":
                live.remove(c)
    out.wait()
    for copy in sends:
        copy.wait_send()


def shards(query_nope, query_rope, latent, rope_key, key_up, value_up, grad_out, group_order):
    ctx, nh, dp = (lax.axis_size(a) for a in ("ctx", "head", "dp"))
    nx = math.isqrt(ctx)
    ny = ctx // nx
    nz = dp // 2
    rows = query_nope.shape[1]
    cols = key_up.shape[1]
    heads = cols // HEAD_DIM
    rope = rope_key.shape[2]
    width = latent.shape[2]
    keys = ctx * rows
    chunk = ny * rows
    half = width // 2
    hw = width // 4
    r1 = hw // nx
    share = width // nh
    factor = 1.0 / math.sqrt(HEAD_DIM + rope)
    dims = (nx, ny, nh, nz, heads, width, rope, factor)
    vmem = pltpu.VMEM
    dma = pltpu.SemaphoreType.DMA
    n3 = max(nx - 1, 1)
    z3 = max(nz - 1, 1)
    h3 = max(nh - 1, 1)
    scratch = [
        vmem((keys, width + 128), BF16),
        vmem((width, keys), BF16),
        vmem((rows, cols), BF16),
        vmem((rows, heads * rope), BF16),
        vmem((width, cols), BF16),
        vmem((width, cols), BF16),
        vmem((rows, cols), BF16),
        vmem((rows, rope), BF16),
        vmem((width + 128, cols), BF16),
        vmem((width, cols), F32),
        vmem((width, cols), BF16),
        vmem((keys, cols), F32),
        vmem((keys, cols), F32),
        vmem((keys, cols), BF16),
        vmem((keys, cols), BF16),
        vmem((chunk, 128), F32),
        vmem((1, cols), F32),
        vmem((1, cols), F32),
        vmem((1, cols), F32),
        vmem((1, cols), F32),
        vmem((width, cols), BF16),
        vmem((width, cols), BF16),
        vmem((cols, width), BF16),
        vmem((cols, width), BF16),
        vmem((keys, width), BF16),
        vmem((n3, chunk, half), BF16),
        vmem((n3, nx, rows, half), BF16),
        vmem((chunk, half), BF16),
        vmem((nx, rows, half), BF16),
        vmem((n3, rows, half), BF16),
        vmem((n3, rows, half), BF16),
        vmem((rows, width), BF16),
        vmem((h3, rows, share), BF16),
        vmem((rows, share), BF16),
        vmem((2, width, cols), BF16),
        vmem((2, width // 2, cols), BF16),
        vmem((2, width // 2, cols), BF16),
        vmem((2, 2, n3, r1, cols), BF16),
        vmem((2, 2, r1, cols), F32),
        vmem((2, 2, n3, r1, cols // ny), F32),
        vmem((2, 2, r1, cols // ny), F32),
        vmem((2, 2, z3, r1 // nz, cols // ny), F32),
        vmem((2, width, cols), BF16),
        dma((7,)), dma((3,)),
        dma((2, 16)), dma((2, ctx)),
        dma((1 + nx, n3)), dma((1 + nx, n3)),
        dma((2, n3)), dma((2, n3)),
        dma((h3,)), dma((h3,)),
        dma((2,)), dma((2,)),
        dma((2, 2, n3)), dma((2, 2, n3)),
        dma((2, 2, n3)), dma((2, 2, n3)),
        dma((2, 2, z3)), dma((2, 2, z3)),
        dma((2, 2, z3)), dma((2, 2, z3)),
        dma((2, 2, n3)), dma((2, 2, n3)),
        dma((2, 2, n3)), dma((2, 2, n3)),
        dma((2,)), dma((2,)),
    ]
    hbm = pl.BlockSpec(memory_space=pl.ANY)
    lat, key_grad, value_grad = pl.pallas_call(
        functools.partial(kernel, dims),
        out_shape=(
            jax.ShapeDtypeStruct((rows, share), BF16),
            jax.ShapeDtypeStruct((width, cols), BF16),
            jax.ShapeDtypeStruct((width, cols), BF16),
        ),
        in_specs=[pl.BlockSpec(memory_space=pltpu.SMEM)] + [hbm] * 7,
        out_specs=(hbm, hbm, hbm),
        scratch_shapes=scratch,
        compiler_params=pltpu.CompilerParams(
            collective_id=0, has_side_effects=True, vmem_limit_bytes=60 * 1024 * 1024
        ),
        cost_estimate=pl.CostEstimate(flops=15_000_000_000, bytes_accessed=8_000_000, transcendentals=2_000_000),
    )(
        group_order, latent[0], rope_key[0], query_nope[0], query_rope[0],
        key_up, value_up, grad_out[0],
    )
    return lat[None], key_grad.astype(F32), value_grad.astype(F32)


def solution(mesh):
    in_specs = (
        P("dp", "ctx", "head"),
        P("dp", "ctx", "head"),
        P("dp", "ctx", None),
        P("dp", "ctx", None),
        P(None, "head"),
        P(None, "head"),
        P("dp", "ctx", "head"),
        P(),
    )
    out_specs = (P("dp", "ctx", "head"), P(None, "head"), P(None, "head"))
    return jax.shard_map(shards, mesh=mesh, in_specs=in_specs, out_specs=out_specs, check_vma=False)
```

time: 899 us -> 99.2 us (0.11)
  waiting for transfers between devices: 696 us -> 0 us
  matrix products: 109 us -> 0 us
  Pallas kernels: 0 us -> 91.8 us
  local copies, waits for them, and re-layouts: 50.2 us -> 2.06 us
  blocking collectives: 22.9 us -> 0 us
  between operations: 13.9 us -> 0.65 us
    psum x1 -> x0, waiting for transfers between devices: 566 us -> none  [shards(): lax.psum((key_local, value_local), ('ctx', 'dp'))]
    dot_general x80 -> x0, matrix products: 109 us -> none  [contract(): lax.dot_general(left_side, right_side, (((left_dim,), (right_dim,)), ((),...]
    reduce_scatter x2 -> x0, waiting for transfers between devices: 104 us -> none  [the longest x1 81.4 us: shards(): lax.psum_scatter(totals, 'ctx', scatter_dimension=1, tiled=True)]
    pallas_call x0 -> x1, Pallas kernels: none -> 91.8 us  [shards(): pl.pallas_call(functools.partial(kernel, dims), out_shape=(jax.ShapeDtype...]
    while x144 -> x0, local copies, waits for them, and re-layouts: 34 us -> none
    all_gather x1 -> x0, waiting for transfers between devices: 25 us -> none  [shards(): lax.all_gather(latent, 'ctx', axis=1, tiled=True)]
    all_gather x1 -> x0, blocking collectives: 22.9 us -> none  [shards(): lax.all_gather(rope_key, 'ctx', axis=1, tiled=True)]
    unnamed x18 -> x6, local copies, waits for them, and re-layouts: 11.9 us -> 2.06 us
  transfers between devices with their start and end apart: 4 -> 0, of which waited for: 4 -> 0; matrix products, arithmetic and copies ran while one was open for 1% -> 0% of each run, Pallas kernels for 0% -> 0%
where the time goes in v1:
time: 99.2 us; the launch traced here: 99 us
  Pallas kernels  91.8 us (93%)
  other arithmetic  4.44 us (4%)
  local copies, waits for them, and re-layouts  2.06 us (2%)
    pallas_call x1, Pallas kernels, shards(): pl.pallas_call(functools.partial(kernel, dims), out_shape=(jax.ShapeDtype...  91.8 us
    convert_element_type x2, other arithmetic, shards(): return (lat[None], key_grad.astype(F32), value_grad.astype(F32))  4.44 us
    unnamed x6, local copies, waits for them, and re-layouts  2.06 us

profile of v1, /device:TPU:1, one launch (start us, length us, event | category | flops | bytes accessed | tf_op | source)
XLA Modules:
  0.0 99.0 jit_solution(9547539770936766646)
XLA Ops:
  0.6 1.4 %copy.11 = bf16[1,128,64]{2,1,0:T(8,128)(2,1)} copy(bf16[1,128,64]{1,2,0:T(8,128)(2,1)} %param.11) | data formatting | bytes 32768 | tf_op args[3]
  2.1 91.8 %shard_map.103 = (bf16[128,128]{1,0:T(8,128)(2,1)}, bf16[512,1024]{1,0:T(8,128)(2,1)}, bf16[512,1024]{1,0:T(8,128)(2,1)}) custom-call(s32[32]{0:T(128)} %refs_0_.1, bf16[128,512]{1,0:T(8,128)(2,1)} %bitcast.10, bf16[128,64]{1,0:T(8,128)(2,1)} %bitcast.6, bf16[128,1024]{1,0:T(8,128)(2,1)} %bitcast.8, bf16[128,512]{1,0:T(8,128)(2,1)} %bitcast.11, ...), custom_call_target="tpu_custom_call" | custom-call | flops 15000000512 | bytes 8000000 | tf_op jit(solution)/shard_map/pallas_call | solution.py:585
  93.9 0.0 copy-start
  93.9 2.9 %convert_element_type.6 = f32[512,1024]{1,0:T(8,128)} convert(bf16[512,1024]{1,0:T(8,128)(2,1)} %get-tuple-element.7) | non-fusion elementwise | flops 524288 | bytes 3145728 | tf_op jit(solution)/shard_map/convert_element_type | solution.py:603
  96.8 0.0 copy-done
  96.8 0.0 copy-start.1
  96.8 1.6 %convert_element_type.7 = f32[512,1024]{1,0:T(8,128)} convert(bf16[512,1024]{1,0:T(8,128)(2,1)S(1)} %copy-done) | non-fusion elementwise | flops 524288 | bytes 3145728 | tf_op jit(solution)/shard_map/convert_element_type | solution.py:603
  98.4 0.0 copy-done.1
  98.4 0.6 copy.13
Async XLA Ops:
  93.9 2.9 %copy-start = (bf16[512,1024]{1,0:T(8,128)(2,1)S(1)}, bf16[512,1024]{1,0:T(8,128)(2,1)}, u32[]{:S(2)}) copy-start(bf16[512,1024]{1,0:T(8,128)(2,1)} %get-tuple-element.8) | copy-start | bytes 3145732
  96.8 1.6 %copy-start.1 = (bf16[128,128]{1,0:T(8,128)(2,1)S(1)}, bf16[128,128]{1,0:T(8,128)(2,1)}, u32[]{:S(2)}) copy-start(bf16[128,128]{1,0:T(8,128)(2,1)} %get-tuple-element.6) | copy-start | bytes 98308

commit v2 on v1

v2 whole, which is shorter than its diff:
```python
import functools
import math

import jax
import jax.numpy as jnp
from jax import lax
from jax.experimental import pallas as pl
from jax.experimental.pallas import tpu as pltpu
from jax.sharding import PartitionSpec as P

HEAD_DIM = 128
GROUP = 64
F32 = jnp.float32
BF16 = jnp.bfloat16
MESH = pl.DeviceIdType.MESH


def dot_nn(left, right):
    return lax.dot_general(left, right, (((1,), (0,)), ((), ())), preferred_element_type=F32)


def dot_nt(left, right):
    return lax.dot_general(left, right, (((1,), (1,)), ((), ())), preferred_element_type=F32)


def dot_tn(left, right):
    return lax.dot_general(left, right, (((0,), (0,)), ((), ())), preferred_element_type=F32)


def mult(value, factor):
    return pl.multiple_of(value * factor, factor)


def kernel(dims, *refs):
    (nx, ny, nh, nz, heads, latent, rope, factor) = dims
    (
        group_ref, lat_ref, rk_ref, qn_ref, qr_ref, ku_ref, vu_ref, go_ref,
        lat_out, key_out, val_out,
        kbuf, lat_t, qn, qr, ku, vu, go, rk,
        q_t, g_t, g_low, score, gprob, prob, dscore,
        bias, peak, peaks, total, inv, rdot,
        o_acc, o_low, gq_low, g_nat, q_nat,
        lsend, l1a, l1b, l2as, l2bs, l2a, l2b, lzs, lzr, lat_v,
        w_own, w_core, w_acc, w1, w1s, w2, w_out,
        in_sem, out_sem, ag_s, ag_r, l_s, l_r, l2_s, l2_r, lz_s, lz_r,
        wc_s, wc_r, w1_s, w1_r, w2_s, w2_r,
        v2_s, v2_r, v1_s, v1_r, vc_s, vc_r, plane,
    ) = refs
    rows = 128
    blocks = nx * ny
    keys = blocks * rows
    cols = heads * HEAD_DIM
    half_lat = latent // 2
    bits = blocks.bit_length() - 1
    chunk = 4 * rows
    chunks = blocks // 4

    ctx = lax.axis_index("ctx")
    head = lax.axis_index("head")
    dp = lax.axis_index("dp")
    zl, core = dp // 2, lax.rem(dp, 2)

    def gray(v):
        return v // 2 * 2 + lax.rem(v // 2 + lax.rem(v, 2), 2)

    def flip(v, off):
        return lax.rem(v // 2 + off // 2, 2) * 2 + lax.rem(lax.rem(v, 2) + off % 2, 2)

    gx, gy = gray(ctx // ny), gray(lax.rem(ctx, ny))

    def block_of(slot):
        return gray(flip(gx, slot // ny)) * ny + gray(flip(gy, slot % ny))

    def at_slot(slot):
        return {"ctx": block_of(slot)}

    def at_x(off):
        return at_slot(off * ny)

    def at_y(off):
        return at_slot(off)

    def at_core():
        return {"dp": zl * 2 + 1 - core}

    def zs(off):
        return lax.rem(zl + off, nz)

    def at_z(off, slot):
        where = {"dp": zs(off) * 2 + core}
        return {**at_slot(slot), **where} if slot else where

    def at_head(off):
        return {"head": lax.rem(head + off, nh)}

    x_offs = list(range(1, nx))
    y_offs = list(range(1, ny))
    partners = (
        [at_slot(1 << t) for t in range(bits)] + [at_core()]
        + [at_z(z, 0) for z in range(1, nz)] + [at_head(o) for o in range(1, nh)]
    )
    order = sorted(range(blocks), key=lambda j: (j.bit_count(), j))
    place_of = {j: i for i, j in enumerate(order)}

    sends = []

    def send(src, dst, ssem, rsem, where):
        copy = pltpu.make_async_remote_copy(
            src_ref=src, dst_ref=dst, send_sem=ssem, recv_sem=rsem,
            device_id=where, device_id_type=MESH,
        )
        copy.start()
        sends.append(copy)

    def arrived(dst, ssem, rsem, where):
        pltpu.make_async_remote_copy(
            src_ref=dst, dst_ref=dst, send_sem=ssem, recv_sem=rsem,
            device_id=where, device_id_type=MESH,
        ).wait_recv()

    barrier = pltpu.get_barrier_semaphore()
    for where in partners:
        pl.semaphore_signal(barrier, inc=1, device_id=where, device_id_type=MESH)

    own_rows = pl.ds(0, rows)
    loads = [
        pltpu.make_async_copy(lat_ref, kbuf.at[own_rows, pl.ds(0, latent)], in_sem.at[0]),
        pltpu.make_async_copy(rk_ref, rk, in_sem.at[1]),
        pltpu.make_async_copy(qn_ref, qn, in_sem.at[2]),
        pltpu.make_async_copy(ku_ref, ku, in_sem.at[3]),
        pltpu.make_async_copy(qr_ref, qr, in_sem.at[4]),
        pltpu.make_async_copy(go_ref, go, in_sem.at[5]),
        pltpu.make_async_copy(vu_ref, vu, in_sem.at[6]),
    ]
    for copy in loads:
        copy.start()

    loads[1].wait()
    spread = lax.broadcasted_iota(jnp.int32, (rope, 128), 0)
    lane = lax.broadcasted_iota(jnp.int32, (rope, 128), 1)
    twice = jnp.where(spread == lax.rem(lane, rope), 1.0, 0.0).astype(BF16)
    kbuf[own_rows, pl.ds(latent, 128)] = dot_tn(rk[...], twice).astype(BF16)
    loads[0].wait()
    pl.semaphore_wait(barrier, len(partners))

    part = rows // bits

    def piece(k, slot):
        return kbuf.at[pl.ds(place_of[slot] * rows + k * part, part)]

    def gather_send(k, slot, step):
        bit = 1 << ((k + step) % bits)
        there = slot ^ bit
        send(piece(k, slot), piece(k, there), ag_s.at[k, there], ag_r.at[k, there], at_slot(bit))

    def last_step(k, slot):
        return max([-1] + [t for t in range(bits) if slot >> ((k + t) % bits) & 1])

    def relay(depth):
        todo = [(last_step(k, j), j, k) for k in range(bits) for j in range(blocks) if j.bit_count() == depth]
        for last, slot, k in sorted(todo):
            arrived(piece(k, slot), ag_s.at[k, slot], ag_r.at[k, slot], at_slot(1))
            for step in range(last + 1, bits):
                gather_send(k, slot, step)

    for step in range(bits):
        for k in range(bits):
            gather_send(k, 0, step)

    for copy in loads[2:]:
        copy.wait()
    row_id = lax.broadcasted_iota(jnp.int32, (128, 128), 0)
    col_id = lax.broadcasted_iota(jnp.int32, (128, 128), 1)
    eye = row_id == col_id

    def head_cols(h):
        return pl.ds(mult(h, 128), 128)

    def project(i, carry):
        for h in (2 * i, 2 * i + 1):
            hc = head_cols(h)
            q_t[pl.ds(0, latent), hc] = dot_nt(ku[:, hc], qn[:, hc]).astype(BF16)
            pick = jnp.where(eye & (row_id // rope == lax.rem(h, 2)), 1.0, 0.0).astype(BF16)
            pair = qr[:, pl.ds(mult(i, 128), 128)]
            q_t[pl.ds(latent, 128), hc] = dot_nt(pick, pair).astype(BF16)
            grad = dot_nt(vu[:, hc], go[:, hc])
            g_t[:, hc] = grad
            g_low[:, hc] = grad.astype(BF16)
        return carry

    lax.fori_loop(0, heads // 2, project, 0)
    relay(1)

    def project_rows(i, carry):
        for h in (2 * i, 2 * i + 1):
            hc = head_cols(h)
            g_nat[hc, :] = dot_nt(go[:, hc], vu[:, hc]).astype(BF16)
            q_nat[hc, :] = (dot_nt(qn[:, hc], ku[:, hc]) * factor).astype(BF16)
        return carry

    lanes = lax.broadcasted_iota(jnp.int32, (GROUP, 128), 1)
    downs = lax.broadcasted_iota(jnp.int32, (GROUP, 128), 0)
    own_low, own_high = group_ref[2 * ctx], group_ref[2 * ctx + 1]
    q_pos = jnp.where(lanes < GROUP, own_low * GROUP + lanes, own_high * GROUP + lanes - GROUP)
    peak[...] = jnp.full(peak.shape, -1e30, F32)
    total[...] = jnp.zeros(total.shape, F32)
    o_acc[...] = jnp.zeros(o_acc.shape, F32)
    ident = jnp.where(eye, 1.0, 0.0).astype(BF16)
    tile = 256
    tiles = cols // tile
    scale = factor * math.log2(math.e)

    def tile_cols(n):
        return pl.ds(mult(n, tile), tile)

    depth = 1
    for i in range(chunks):
        while depth < max(j.bit_count() for j in order[4 * i:4 * i + 4]):
            depth += 1
            relay(depth)
        span = pl.ds(i * chunk, chunk)
        for b in range(4):
            block = block_of(order[4 * i + b])
            for g in range(2):
                k_pos = group_ref[2 * block + g] * GROUP + downs
                bias[pl.ds(b * rows + g * GROUP, GROUP), :] = jnp.where(k_pos <= q_pos, 0.0, -jnp.inf)
        for b in range(latent // 128):
            turned = dot_nt(ident, kbuf[span, pl.ds(b * 128, 128)])
            lat_t[pl.ds(b * 128, 128), span] = turned.astype(BF16)

        def tile_scores(n, span=span):
            return dot_nn(kbuf[span, :], q_t[:, n * tile:(n + 1) * tile])

        s = tile_scores(0)
        for n in range(tiles):
            tc = pl.ds(n * tile, tile)
            ahead = tile_scores(n + 1) if n + 1 < tiles else None
            gprob[span, tc] = dot_nn(kbuf[span, pl.ds(0, latent)], g_low[:, tc])
            s = s + jnp.concatenate([bias[...]] * (tile // 128), axis=1)
            old = peak[:, tc]
            new = jnp.maximum(old, jnp.max(s, axis=0, keepdims=True))
            p = jnp.exp2((s - new) * scale)
            fade = jnp.exp2((old - new) * scale)
            score[span, tc] = p
            total[:, tc] = total[:, tc] * fade + jnp.sum(p, axis=0, keepdims=True)
            peak[:, tc] = new
            peaks[pl.ds(i, 1), tc] = new
            o_acc[:, tc] = o_acc[:, tc] * fade + dot_nn(lat_t[:, span], p.astype(BF16))
            s = ahead
        if i == 0:
            lax.fori_loop(0, heads // 2, project_rows, 0)
        if i + 1 < chunks and depth < bits:
            depth += 1
            relay(depth)

    for z in range(1, nz):
        pl.semaphore_signal(plane, inc=1, device_id=at_z(z, 0), device_id_type=MESH)
    inv[...] = 1.0 / total[...]

    def read_out(n, carry):
        tc = tile_cols(n)
        o = o_acc[:, tc] * inv[:, tc]
        o_low[:, tc] = o.astype(BF16)
        rdot[:, tc] = jnp.sum(g_t[:, tc] * o, axis=0, keepdims=True)
        return carry

    lax.fori_loop(0, tiles, read_out, 0)
    for i in range(chunks):
        peaks[pl.ds(i, 1), :] = jnp.exp2((peaks[pl.ds(i, 1), :] - peak[...]) * scale) * inv[...]

    core_rows = latent // 2
    hw = core_rows // 2

    def chain(w):
        first = ((nx, gx, at_x, x_offs, ny), (ny, gy, at_y, y_offs, 1))
        base = core * core_rows

        def cut(s):
            (n1, i1, a1, o1, u1), (n2, i2, a2, o2, u2) = first[s], first[1 - s]
            pairs = [(o, z) for z in range(nz) for o in range(n2) if o or z]
            return n1, i1, a1, o1, n2, i2, u2, pairs, hw // n1, hw // n1 // nz, cols // n2

        def peer(o, z, u2):
            return at_z(z, o * u2) if z else at_slot(o * u2)

        send(
            w_own.at[w, pl.ds(mult(1 - core, core_rows), core_rows)], w_core.at[w],
            wc_s.at[w], wc_r.at[w], at_core(),
        )
        yield
        arrived(w_core.at[w], wc_s.at[w], wc_r.at[w], at_core())
        mine = w_own[w, pl.ds(mult(core, core_rows), core_rows), :].astype(F32)
        w_acc[w] = (mine + w_core[w].astype(F32)).astype(BF16)
        for s in range(2):
            n1, i1, a1, o1, n2, i2, u2, pairs, r, rz, c = cut(s)
            for o in o1:
                send(
                    w_acc.at[w, pl.ds(pl.multiple_of(s * hw + flip(i1, o) * r, r), r)], w1.at[w, s, o - 1],
                    w1_s.at[w, s, o - 1], w1_r.at[w, s, o - 1], a1(o),
                )
        yield
        for s in range(2):
            n1, i1, a1, o1, n2, i2, u2, pairs, r, rz, c = cut(s)
            acc = w_acc[w, pl.ds(pl.multiple_of(s * hw + i1 * r, r), r), :].astype(F32)
            for o in o1:
                arrived(w1.at[w, s, o - 1], w1_s.at[w, s, o - 1], w1_r.at[w, s, o - 1], a1(o))
                acc = acc + w1[w, s, o - 1].astype(F32)
            w1s[w, s] = acc
            if w == 0 and s == 0 and nz > 1:
                pl.semaphore_wait(plane, nz - 1)
            for o, z in pairs:
                slot = z * n2 + o
                send(
                    w1s.at[w, s, pl.ds(mult(zs(z), rz), rz), pl.ds(mult(flip(i2, o), c), c)],
                    w2.at[w, s, slot], w2_s.at[w, s, slot], w2_r.at[w, s, slot], peer(o, z, u2),
                )
        yield

        def place(s, top, left, height, width):
            start = pl.multiple_of(base + s * hw + top, 16)
            return w_out.at[w, pl.ds(start, height), pl.ds(left, width)]

        for s in range(2):
            n1, i1, a1, o1, n2, i2, u2, pairs, r, rz, c = cut(s)
            acc = w1s[w, s, pl.ds(mult(zl, rz), rz), pl.ds(mult(i2, c), c)]
            for o, z in pairs:
                slot = z * n2 + o
                arrived(w2.at[w, s, slot], w2_s.at[w, s, slot], w2_r.at[w, s, slot], peer(o, z, u2))
                acc = acc + w2[w, s, slot]
            spot = place(s, i1 * r + zl * rz, mult(i2, c), rz, c)
            spot[...] = acc.astype(BF16)
            for o, z in pairs:
                slot = z * n2 + o
                send(spot, spot, v2_s.at[w, s, slot], v2_r.at[w, s, slot], peer(o, z, u2))
        yield
        for s in range(2):
            n1, i1, a1, o1, n2, i2, u2, pairs, r, rz, c = cut(s)
            for o, z in pairs:
                slot = z * n2 + o
                spot = place(s, i1 * r + zs(nz - z) * rz, mult(flip(i2, o), c), rz, c)
                arrived(spot, v2_s.at[w, s, slot], v2_r.at[w, s, slot], peer(o, z, u2))
            spot = place(s, i1 * r, 0, r, cols)
            for o in o1:
                send(spot, spot, v1_s.at[w, s, o - 1], v1_r.at[w, s, o - 1], a1(o))
        yield
        for s in range(2):
            n1, i1, a1, o1, n2, i2, u2, pairs, r, rz, c = cut(s)
            for o in o1:
                spot = place(s, flip(i1, o) * r, 0, r, cols)
                arrived(spot, v1_s.at[w, s, o - 1], v1_r.at[w, s, o - 1], a1(o))
        spot = w_out.at[w, pl.ds(mult(core, core_rows), core_rows)]
        send(spot, spot, vc_s.at[w], vc_r.at[w], at_core())
        yield
        spot = w_out.at[w, pl.ds(mult(1 - core, core_rows), core_rows)]
        arrived(spot, vc_s.at[w], vc_r.at[w], at_core())
        out = pltpu.make_async_copy(w_out.at[w], (val_out, key_out)[w], out_sem.at[w])
        out.start()
        yield
        out.wait()
        yield

    def value_head(h, carry):
        hc = head_cols(h)
        w_own[0, :, hc] = dot_nn(o_low[:, hc], go[:, hc]).astype(BF16)
        return carry

    lax.fori_loop(0, heads, value_head, 0)
    value_chain, key_chain = chain(0), chain(1)
    next(value_chain)

    step = 128

    def grade(j, carry, i=0):
        span = pl.ds(pl.multiple_of(i * chunk + j * step, step), step)
        p = score[span, :] * peaks[pl.ds(i, 1), :]
        prob[span, :] = p.astype(BF16)
        dscore[span, :] = (p * (gprob[span, :] - rdot[...])).astype(BF16)
        return carry

    for i in range(chunks):
        lax.fori_loop(0, chunk // step, functools.partial(grade, i=i), 0)

    def query_grad(n):
        tc = pl.ds(n * tile, tile)
        gq_low[:, tc] = (dot_nn(lat_t[...], dscore[:, tc]) * factor).astype(BF16)

    def key_head(h, carry):
        hc = head_cols(h)
        w_own[1, :, hc] = dot_nn(gq_low[:, hc], qn[:, hc]).astype(BF16)
        return carry

    def latent_chunk(i):
        span = pl.ds(i * chunk, chunk)
        for n in range(2):
            cs = pl.ds(n * half_lat, half_lat)
            part_sum = dot_nn(prob[span, :], g_nat[:, cs]) + dot_nn(dscore[span, :], q_nat[:, cs])
            lsend[span, cs] = part_sum.astype(BF16)
        for slot in reversed(order[4 * i:4 * i + 4]):
            jx, jy = slot // ny, slot % ny
            block = pl.ds(place_of[slot] * rows, rows)
            if jx:
                send(
                    lsend.at[block, pl.ds(0, half_lat)], l1a.at[jx - 1, jy],
                    l_s.at[0, jx - 1, jy], l_r.at[0, jx - 1, jy], at_x(jx),
                )
            if jy:
                send(
                    lsend.at[block, pl.ds(half_lat, half_lat)], l1b.at[jy - 1, jx],
                    l_s.at[1, jy - 1, jx], l_r.at[1, jy - 1, jx], at_y(jy),
                )

    next(value_chain)
    latent_chunk(chunks - 1)
    for n in range(tiles):
        query_grad(n)
    lax.fori_loop(0, heads, key_head, 0)
    next(key_chain)
    next(value_chain)
    rest = list(reversed(range(chunks - 1)))
    for n, i in enumerate(rest):
        latent_chunk(i)
        if n == 0:
            next(key_chain)
        if n == 1:
            next(value_chain)
    for _ in range(2 - len(rest)):
        next((value_chain, key_chain)[_])

    next(key_chain)
    next(value_chain)
    for jy in y_offs + [0]:
        block = pl.ds(place_of[jy] * rows, rows)
        acc = lsend[block, pl.ds(0, half_lat)].astype(F32)
        for jx in x_offs:
            arrived(l1a.at[jx - 1, jy], l_s.at[0, jx - 1, jy], l_r.at[0, jx - 1, jy], at_x(jx))
            acc = acc + l1a[jx - 1, jy].astype(F32)
        l2as[jy] = acc.astype(BF16)
        if jy:
            send(l2as.at[jy], l2a.at[jy - 1], l2_s.at[0, jy - 1], l2_r.at[0, jy - 1], at_y(jy))
    for jx in x_offs + [0]:
        block = pl.ds(place_of[jx * ny] * rows, rows)
        acc = lsend[block, pl.ds(half_lat, half_lat)].astype(F32)
        for jy in y_offs:
            arrived(l1b.at[jy - 1, jx], l_s.at[1, jy - 1, jx], l_r.at[1, jy - 1, jx], at_y(jy))
            acc = acc + l1b[jy - 1, jx].astype(F32)
        l2bs[jx] = acc.astype(BF16)
        if jx:
            send(l2bs.at[jx], l2b.at[jx - 1], l2_s.at[1, jx - 1], l2_r.at[1, jx - 1], at_x(jx))
    next(key_chain)

    acc = l2as[0].astype(F32)
    for o in y_offs:
        arrived(l2a.at[o - 1], l2_s.at[0, o - 1], l2_r.at[0, o - 1], at_y(o))
        acc = acc + l2a[o - 1].astype(F32)
    lzs[:, pl.ds(0, half_lat)] = acc.astype(BF16)
    acc = l2bs[0].astype(F32)
    for o in x_offs:
        arrived(l2b.at[o - 1], l2_s.at[1, o - 1], l2_r.at[1, o - 1], at_x(o))
        acc = acc + l2b[o - 1].astype(F32)
    lzs[:, pl.ds(half_lat, half_lat)] = acc.astype(BF16)
    share = latent // nh
    for o in range(1, nh):
        send(
            lzs.at[:, pl.ds(mult(lax.rem(head + o, nh), share), share)], lzr.at[o - 1],
            lz_s.at[o - 1], lz_r.at[o - 1], at_head(o),
        )
    next(key_chain)
    next(value_chain)
    acc = lzs[:, pl.ds(mult(head, share), share)].astype(F32)
    for o in range(1, nh):
        arrived(lzr.at[o - 1], lz_s.at[o - 1], lz_r.at[o - 1], at_head(o))
        acc = acc + lzr[o - 1].astype(F32)
    lat_v[...] = acc.astype(BF16)
    out = pltpu.make_async_copy(lat_v, lat_out, out_sem.at[2])
    out.start()
    live = [value_chain, key_chain]
    while live:
        for c in list(live):
            if next(c, "end") == "end":
                live.remove(c)
    out.wait()
    for copy in sends:
        copy.wait_send()


def shards(query_nope, query_rope, latent, rope_key, key_up, value_up, grad_out, group_order):
    ctx, nh, dp = (lax.axis_size(a) for a in ("ctx", "head", "dp"))
    nx = math.isqrt(ctx)
    ny = ctx // nx
    nz = dp // 2
    rows = query_nope.shape[1]
    cols = key_up.shape[1]
    heads = cols // HEAD_DIM
    rope = rope_key.shape[2]
    width = latent.shape[2]
    keys = ctx * rows
    bits = ctx.bit_length() - 1
    half = width // 2
    hw = width // 4
    r1 = hw // nx
    share = width // nh
    factor = 1.0 / math.sqrt(HEAD_DIM + rope)
    dims = (nx, ny, nh, nz, heads, width, rope, factor)
    vmem = pltpu.VMEM
    dma = pltpu.SemaphoreType.DMA
    n3 = max(nx - 1, 1)
    h3 = max(nh - 1, 1)
    scratch = [
        vmem((keys, width + 128), BF16),
        vmem((width, keys), BF16),
        vmem((rows, cols), BF16),
        vmem((rows, heads * rope), BF16),
        vmem((width, cols), BF16),
        vmem((width, cols), BF16),
        vmem((rows, cols), BF16),
        vmem((rope, rows), BF16),
        vmem((width + 128, cols), BF16),
        vmem((width, cols), F32),
        vmem((width, cols), BF16),
        vmem((keys, cols), F32),
        vmem((keys, cols), F32),
        vmem((keys, cols), BF16),
        vmem((keys, cols), BF16),
        vmem((512, 128), F32),
        vmem((1, cols), F32),
        vmem((8, cols), F32),
        vmem((1, cols), F32),
        vmem((1, cols), F32),
        vmem((1, cols), F32),
        vmem((width, cols), F32),
        vmem((width, cols), BF16),
        vmem((width, cols), BF16),
        vmem((cols, width), BF16),
        vmem((cols, width), BF16),
        vmem((keys, width), BF16),
        vmem((n3, ny, rows, half), BF16),
        vmem((n3, nx, rows, half), BF16),
        vmem((ny, rows, half), BF16),
        vmem((nx, rows, half), BF16),
        vmem((n3, rows, half), BF16),
        vmem((n3, rows, half), BF16),
        vmem((rows, width), BF16),
        vmem((h3, rows, share), BF16),
        vmem((rows, share), BF16),
        vmem((2, width, cols), BF16),
        vmem((2, width // 2, cols), BF16),
        vmem((2, width // 2, cols), BF16),
        vmem((2, 2, n3, r1, cols), BF16),
        vmem((2, 2, r1, cols), F32),
        vmem((2, 2, ny * nz, r1 // nz, cols // ny), F32),
        vmem((2, width, cols), BF16),
        dma((7,)), dma((3,)),
        dma((bits, ctx)), dma((bits, ctx)),
        dma((2, n3, nx)), dma((2, n3, nx)),
        dma((2, n3)), dma((2, n3)),
        dma((h3,)), dma((h3,)),
        dma((2,)), dma((2,)),
        dma((2, 2, n3)), dma((2, 2, n3)),
        dma((2, 2, ny * nz)), dma((2, 2, ny * nz)),
        dma((2, 2, ny * nz)), dma((2, 2, ny * nz)),
        dma((2, 2, n3)), dma((2, 2, n3)),
        dma((2,)), dma((2,)),
        pltpu.SemaphoreType.REGULAR,
    ]
    hbm = pl.BlockSpec(memory_space=pl.ANY)
    lat, key_grad, value_grad = pl.pallas_call(
        functools.partial(kernel, dims),
        out_shape=(
            jax.ShapeDtypeStruct((rows, share), BF16),
            jax.ShapeDtypeStruct((width, cols), BF16),
            jax.ShapeDtypeStruct((width, cols), BF16),
        ),
        in_specs=[pl.BlockSpec(memory_space=pltpu.SMEM)] + [hbm] * 7,
        out_specs=(hbm, hbm, hbm),
        scratch_shapes=scratch,
        compiler_params=pltpu.CompilerParams(
            collective_id=0, has_side_effects=True, vmem_limit_bytes=60 * 1024 * 1024
        ),
        cost_estimate=pl.CostEstimate(flops=15_000_000_000, bytes_accessed=8_000_000, transcendentals=2_000_000),
    )(
        group_order, latent[0], rope_key[0].T, query_nope[0], query_rope[0],
        key_up, value_up, grad_out[0],
    )
    return lat[None], key_grad.astype(F32), value_grad.astype(F32)


def solution(mesh):
    in_specs = (
        P("dp", "ctx", "head"),
        P("dp", "ctx", "head"),
        P("dp", "ctx", None),
        P("dp", "ctx", None),
        P(None, "head"),
        P(None, "head"),
        P("dp", "ctx", "head"),
        P(),
    )
    out_specs = (P("dp", "ctx", "head"), P(None, "head"), P(None, "head"))
    return jax.shard_map(shards, mesh=mesh, in_specs=in_specs, out_specs=out_specs, check_vma=False)
```

time: 99.2 us -> 88.6 us (0.89)
  Pallas kernels: 91.8 us -> 82.7 us
  local copies, waits for them, and re-layouts: 2.06 us -> 0.62 us
    pallas_call x1, Pallas kernels: 91.8 us -> 82.7 us  [shards(): pl.pallas_call(functools.partial(kernel, dims), out_shape=(jax.ShapeDtype...]
    unnamed x6 -> x5, local copies, waits for them, and re-layouts: 2.06 us -> 0.62 us
where the time goes in v2:
time: 88.6 us; the launch traced here: 88.5 us
  Pallas kernels  82.7 us (93%)
  other arithmetic  4.44 us (5%)
    pallas_call x1, Pallas kernels, shards(): pl.pallas_call(functools.partial(kernel, dims), out_shape=(jax.ShapeDtype...  82.7 us
    convert_element_type x2, other arithmetic, shards(): return (lat[None], key_grad.astype(F32), value_grad.astype(F32))  4.44 us

profile of v2, /device:TPU:1, one launch (start us, length us, event | category | flops | bytes accessed | tf_op | source)
XLA Modules:
  0.0 88.5 jit_solution(9682450570327124172)
XLA Ops:
  0.6 82.7 %shard_map.103 = (bf16[128,128]{1,0:T(8,128)(2,1)}, bf16[512,1024]{1,0:T(8,128)(2,1)}, bf16[512,1024]{1,0:T(8,128)(2,1)}) custom-call(s32[32]{0:T(128)} %refs_0_.1, bf16[128,512]{1,0:T(8,128)(2,1)} %bitcast.11, bf16[64,128]{1,0:T(8,128)(2,1)} %bitcast.13, bf16[128,1024]{1,0:T(8,128)(2,1)} %bitcast.9, bf16[128,512]{1,0:T(8,128)(2,1)} %bitcast.12, ...), custom_call_target="tpu_custom_call" | custom-call | flops 15000000512 | bytes 8000000 | tf_op jit(solution)/shard_map/pallas_call | solution.py:566
  83.4 0.0 copy-start
  83.4 2.9 %convert_element_type.6 = f32[512,1024]{1,0:T(8,128)} convert(bf16[512,1024]{1,0:T(8,128)(2,1)} %get-tuple-element.7) | non-fusion elementwise | flops 524288 | bytes 3145728 | tf_op jit(solution)/shard_map/convert_element_type | solution.py:584
  86.3 0.0 copy-done
  86.3 0.0 copy-start.1
  86.3 1.6 %convert_element_type.7 = f32[512,1024]{1,0:T(8,128)} convert(bf16[512,1024]{1,0:T(8,128)(2,1)S(1)} %copy-done) | non-fusion elementwise | flops 524288 | bytes 3145728 | tf_op jit(solution)/shard_map/convert_element_type | solution.py:584
  87.8 0.0 copy-done.1
  87.8 0.6 copy.12
Async XLA Ops:
  83.4 2.9 %copy-start = (bf16[512,1024]{1,0:T(8,128)(2,1)S(1)}, bf16[512,1024]{1,0:T(8,128)(2,1)}, u32[]{:S(2)}) copy-start(bf16[512,1024]{1,0:T(8,128)(2,1)} %get-tuple-element.8) | copy-start | bytes 3145732
  86.3 1.6 %copy-start.1 = (bf16[128,128]{1,0:T(8,128)(2,1)S(1)}, bf16[128,128]{1,0:T(8,128)(2,1)}, u32[]{:S(2)}) copy-start(bf16[128,128]{1,0:T(8,128)(2,1)} %get-tuple-element.6) | copy-start | bytes 98308

commit v3 on v2

--- a/solution.py
+++ b/solution.py
@@ -40,9 +40,9 @@
         q_t, g_t, g_low, score, gprob, prob, dscore,
         bias, peak, peaks, total, inv, rdot,
         o_acc, o_low, gq_low, g_nat, q_nat,
-        lsend, l1a, l1b, l2as, l2bs, l2a, l2b, lzs, lzr, lat_v,
+        lsend, lrecv, lzs, lzr, lat_v,
         w_own, w_core, w_acc, w1, w1s, w2, w_out,
-        in_sem, out_sem, ag_s, ag_r, l_s, l_r, l2_s, l2_r, lz_s, lz_r,
+        in_sem, out_sem, ag_s, ag_r, l_s, l_r, lz_s, lz_r,
         wc_s, wc_r, w1_s, w1_r, w2_s, w2_r,
         v2_s, v2_r, v1_s, v1_r, vc_s, vc_r, plane,
     ) = refs
@@ -204,7 +204,6 @@
     q_pos = jnp.where(lanes < GROUP, own_low * GROUP + lanes, own_high * GROUP + lanes - GROUP)
     peak[...] = jnp.full(peak.shape, -1e30, F32)
     total[...] = jnp.zeros(total.shape, F32)
-    o_acc[...] = jnp.zeros(o_acc.shape, F32)
     ident = jnp.where(eye, 1.0, 0.0).astype(BF16)
     tile = 256
     tiles = cols // tile
@@ -229,24 +228,25 @@
             lat_t[pl.ds(b * 128, 128), span] = turned.astype(BF16)
 
         def tile_scores(n, span=span):
-            return dot_nn(kbuf[span, :], q_t[:, n * tile:(n + 1) * tile])
-
-        s = tile_scores(0)
+            s = dot_nn(kbuf[span, :], q_t[:, n * tile:(n + 1) * tile])
+            return s + jnp.concatenate([bias[...]] * (tile // 128), axis=1)
+
+        score[:, 0:tile] = tile_scores(0)
         for n in range(tiles):
             tc = pl.ds(n * tile, tile)
-            ahead = tile_scores(n + 1) if n + 1 < tiles else None
+            if n + 1 < tiles:
+                score[:, (n + 1) * tile:(n + 2) * tile] = tile_scores(n + 1)
             gprob[span, tc] = dot_nn(kbuf[span, pl.ds(0, latent)], g_low[:, tc])
-            s = s + jnp.concatenate([bias[...]] * (tile // 128), axis=1)
             old = peak[:, tc]
-            new = jnp.maximum(old, jnp.max(s, axis=0, keepdims=True))
-            p = jnp.exp2((s - new) * scale)
+            new = jnp.maximum(old, jnp.max(score[:, tc], axis=0, keepdims=True))
+            p = jnp.exp2((score[:, tc] - new) * scale)
+            prob[span, tc] = p.astype(BF16)
             fade = jnp.exp2((old - new) * scale)
-            score[span, tc] = p
             total[:, tc] = total[:, tc] * fade + jnp.sum(p, axis=0, keepdims=True)
             peak[:, tc] = new
             peaks[pl.ds(i, 1), tc] = new
-            o_acc[:, tc] = o_acc[:, tc] * fade + dot_nn(lat_t[:, span], p.astype(BF16))
-            s = ahead
+            o = dot_nn(lat_t[:, span], prob[span, tc])
+            o_acc[:, tc] = o if i == 0 else o_acc[:, tc] * fade + o
         if i == 0:
             lax.fori_loop(0, heads // 2, project_rows, 0)
         if i + 1 < chunks and depth < bits:
@@ -316,6 +316,13 @@
                 )
         yield
 
+        out_ref = (val_out, key_out)[w]
+
+        def to_core(s, o):
+            n1, i1, a1, o1, n2, i2, u2, pairs, r, rz, c = cut(s)
+            span = pl.ds(pl.multiple_of(base + s * hw + flip(i1, o) * r, 16), r)
+            send(w_out.at[w, span], out_ref.at[span], vc_s.at[w, s, o], vc_r.at[w, s, o], at_core())
+
         def place(s, top, left, height, width):
             start = pl.multiple_of(base + s * hw + top, 16)
             return w_out.at[w, pl.ds(start, height), pl.ds(left, width)]
@@ -342,21 +349,24 @@
             spot = place(s, i1 * r, 0, r, cols)
             for o in o1:
                 send(spot, spot, v1_s.at[w, s, o - 1], v1_r.at[w, s, o - 1], a1(o))
+            to_core(s, 0)
         yield
         for s in range(2):
             n1, i1, a1, o1, n2, i2, u2, pairs, r, rz, c = cut(s)
             for o in o1:
                 spot = place(s, flip(i1, o) * r, 0, r, cols)
                 arrived(spot, v1_s.at[w, s, o - 1], v1_r.at[w, s, o - 1], a1(o))
-        spot = w_out.at[w, pl.ds(mult(core, core_rows), core_rows)]
-        send(spot, spot, vc_s.at[w], vc_r.at[w], at_core())
+                to_core(s, o)
+        span = pl.ds(mult(core, core_rows), core_rows)
+        own = pltpu.make_async_copy(w_out.at[w, span], out_ref.at[span], out_sem.at[w])
+        own.start()
         yield
-        spot = w_out.at[w, pl.ds(mult(1 - core, core_rows), core_rows)]
-        arrived(spot, vc_s.at[w], vc_r.at[w], at_core())
-        out = pltpu.make_async_copy(w_out.at[w], (val_out, key_out)[w], out_sem.at[w])
-        out.start()
-        yield
-        out.wait()
+        for s in range(2):
+            n1, i1, a1, o1, n2, i2, u2, pairs, r, rz, c = cut(s)
+            for o in [0] + o1:
+                span = pl.ds(pl.multiple_of((1 - core) * core_rows + s * hw + flip(i1, o) * r, 16), r)
+                arrived(out_ref.at[span], vc_s.at[w, s, o], vc_r.at[w, s, o], at_core())
+        own.wait()
         yield
 
     def value_head(h, carry):
@@ -372,7 +382,7 @@
 
     def grade(j, carry, i=0):
         span = pl.ds(pl.multiple_of(i * chunk + j * step, step), step)
-        p = score[span, :] * peaks[pl.ds(i, 1), :]
+        p = prob[span, :].astype(F32) * peaks[pl.ds(i, 1), :]
         prob[span, :] = p.astype(BF16)
         dscore[span, :] = (p * (gprob[span, :] - rdot[...])).astype(BF16)
         return carry
@@ -389,83 +399,93 @@
         w_own[1, :, hc] = dot_nn(gq_low[:, hc], qn[:, hc]).astype(BF16)
         return carry
 
-    def latent_chunk(i):
-        span = pl.ds(i * chunk, chunk)
-        for n in range(2):
-            cs = pl.ds(n * half_lat, half_lat)
+    if bits == 4:
+        stages = (((0,), (1,), (2, 3)), ((2,), (3,), (0, 1)), ((1,), (0,), (2, 3)), ((3,), (2,), (0, 1)))
+    else:
+        stages = (((0,), (1,)), ((1,), (0,)), ((0,), (1,)), ((1,), (0,)))
+    width = latent // 4
+    round_of = {slot: chunks - 1 - place_of[slot] // 4 for slot in range(blocks)}
+
+    def masks(k):
+        return [sum(1 << t for t in group) for group in stages[k]]
+
+    def stage_of(k, slot):
+        return next((t for t, m in enumerate(masks(k)) if slot & m), len(stages[k]))
+
+    def sources(k, slot):
+        return [
+            (slot | h, h) for m in masks(k)[:stage_of(k, slot)] for h in range(1, blocks) if h & m == h
+        ]
+
+    def ready(k, slot):
+        return max([round_of[slot]] + [ready(k, src) + 1 for src, _ in sources(k, slot)])
+
+    def latent_piece(k, slot):
+        return lsend.at[pl.ds(place_of[slot] * rows, rows), pl.ds(k * width, width)]
+
+    def latent_sum(k, slot):
+        acc = latent_piece(k, slot)[...].astype(F32)
+        for src, hop in sources(k, slot):
+            arrived(lrecv.at[k, src], l_s.at[k, src], l_r.at[k, src], at_slot(hop))
+            acc = acc + lrecv[k, src].astype(F32)
+        return acc
+
+    def latent_send(k, slot):
+        if sources(k, slot):
+            latent_piece(k, slot)[...] = latent_sum(k, slot).astype(BF16)
+        hop = slot & masks(k)[stage_of(k, slot)]
+        send(latent_piece(k, slot), lrecv.at[k, slot], l_s.at[k, slot], l_r.at[k, slot], at_slot(hop))
+
+    def latent_chunk(n):
+        span = pl.ds((chunks - 1 - n) * chunk, chunk)
+        for c in range(2):
+            cs = pl.ds(c * half_lat, half_lat)
             part_sum = dot_nn(prob[span, :], g_nat[:, cs]) + dot_nn(dscore[span, :], q_nat[:, cs])
             lsend[span, cs] = part_sum.astype(BF16)
-        for slot in reversed(order[4 * i:4 * i + 4]):
-            jx, jy = slot // ny, slot % ny
-            block = pl.ds(place_of[slot] * rows, rows)
-            if jx:
-                send(
-                    lsend.at[block, pl.ds(0, half_lat)], l1a.at[jx - 1, jy],
-                    l_s.at[0, jx - 1, jy], l_r.at[0, jx - 1, jy], at_x(jx),
-                )
-            if jy:
-                send(
-                    lsend.at[block, pl.ds(half_lat, half_lat)], l1b.at[jy - 1, jx],
-                    l_s.at[1, jy - 1, jx], l_r.at[1, jy - 1, jx], at_y(jy),
-                )
-
-    next(value_chain)
-    latent_chunk(chunks - 1)
+
+    def latent_sends(n):
+        todo = [
+            (stage_of(k, j), -place_of[j], k, j)
+            for j in range(1, blocks) for k in range(4) if min(ready(k, j), chunks - 1) == n
+        ]
+        for _, _, k, j in sorted(todo):
+            latent_send(k, j)
+
     for n in range(tiles):
         query_grad(n)
+    next(value_chain)
     lax.fori_loop(0, heads, key_head, 0)
     next(key_chain)
-    next(value_chain)
-    rest = list(reversed(range(chunks - 1)))
-    for n, i in enumerate(rest):
-        latent_chunk(i)
-        if n == 0:
-            next(key_chain)
-        if n == 1:
-            next(value_chain)
-    for _ in range(2 - len(rest)):
-        next((value_chain, key_chain)[_])
-
+    latent_chunk(0)
+    next(key_chain)
+    latent_sends(0)
+    if chunks > 1:
+        latent_chunk(1)
+        next(value_chain)
+        latent_sends(1)
+        latent_chunk(2)
+        latent_sends(2)
+        next(key_chain)
+        latent_chunk(3)
+        next(value_chain)
+        latent_sends(3)
+    else:
+        next(value_chain)
+        next(key_chain)
+        next(value_chain)
     next(key_chain)
     next(value_chain)
-    for jy in y_offs + [0]:
-        block = pl.ds(place_of[jy] * rows, rows)
-        acc = lsend[block, pl.ds(0, half_lat)].astype(F32)
-        for jx in x_offs:
-            arrived(l1a.at[jx - 1, jy], l_s.at[0, jx - 1, jy], l_r.at[0, jx - 1, jy], at_x(jx))
-            acc = acc + l1a[jx - 1, jy].astype(F32)
-        l2as[jy] = acc.astype(BF16)
-        if jy:
-            send(l2as.at[jy], l2a.at[jy - 1], l2_s.at[0, jy - 1], l2_r.at[0, jy - 1], at_y(jy))
-    for jx in x_offs + [0]:
-        block = pl.ds(place_of[jx * ny] * rows, rows)
-        acc = lsend[block, pl.ds(half_lat, half_lat)].astype(F32)
-        for jy in y_offs:
-            arrived(l1b.at[jy - 1, jx], l_s.at[1, jy - 1, jx], l_r.at[1, jy - 1, jx], at_y(jy))
-            acc = acc + l1b[jy - 1, jx].astype(F32)
-        l2bs[jx] = acc.astype(BF16)
-        if jx:
-            send(l2bs.at[jx], l2b.at[jx - 1], l2_s.at[1, jx - 1], l2_r.at[1, jx - 1], at_x(jx))
     next(key_chain)
-
-    acc = l2as[0].astype(F32)
-    for o in y_offs:
-        arrived(l2a.at[o - 1], l2_s.at[0, o - 1], l2_r.at[0, o - 1], at_y(o))
-        acc = acc + l2a[o - 1].astype(F32)
-    lzs[:, pl.ds(0, half_lat)] = acc.astype(BF16)
-    acc = l2bs[0].astype(F32)
-    for o in x_offs:
-        arrived(l2b.at[o - 1], l2_s.at[1, o - 1], l2_r.at[1, o - 1], at_x(o))
-        acc = acc + l2b[o - 1].astype(F32)
-    lzs[:, pl.ds(half_lat, half_lat)] = acc.astype(BF16)
+    for k in range(4):
+        lzs[:, pl.ds(k * width, width)] = latent_sum(k, 0).astype(BF16)
     share = latent // nh
     for o in range(1, nh):
         send(
             lzs.at[:, pl.ds(mult(lax.rem(head + o, nh), share), share)], lzr.at[o - 1],
             lz_s.at[o - 1], lz_r.at[o - 1], at_head(o),
         )
+    next(value_chain)
     next(key_chain)
-    next(value_chain)
     acc = lzs[:, pl.ds(mult(head, share), share)].astype(F32)
     for o in range(1, nh):
         arrived(lzr.at[o - 1], lz_s.at[o - 1], lz_r.at[o - 1], at_head(o))
@@ -483,6 +503,12 @@
         copy.wait_send()
 
 
+def widen(lat_ref, key_ref, value_ref, lat_out, key_out, value_out):
+    lat_out[...] = lat_ref[...]
+    key_out[...] = key_ref[...].astype(F32)
+    value_out[...] = value_ref[...].astype(F32)
+
+
 def shards(query_nope, query_rope, latent, rope_key, key_up, value_up, grad_out, group_order):
     ctx, nh, dp = (lax.axis_size(a) for a in ("ctx", "head", "dp"))
     nx = math.isqrt(ctx)
@@ -495,7 +521,6 @@
     width = latent.shape[2]
     keys = ctx * rows
     bits = ctx.bit_length() - 1
-    half = width // 2
     hw = width // 4
     r1 = hw // nx
     share = width // nh
@@ -517,7 +542,7 @@
         vmem((width + 128, cols), BF16),
         vmem((width, cols), F32),
         vmem((width, cols), BF16),
-        vmem((keys, cols), F32),
+        vmem((512, cols), F32),
         vmem((keys, cols), F32),
         vmem((keys, cols), BF16),
         vmem((keys, cols), BF16),
@@ -533,12 +558,7 @@
         vmem((cols, width), BF16),
         vmem((cols, width), BF16),
         vmem((keys, width), BF16),
-        vmem((n3, ny, rows, half), BF16),
-        vmem((n3, nx, rows, half), BF16),
-        vmem((ny, rows, half), BF16),
-        vmem((nx, rows, half), BF16),
-        vmem((n3, rows, half), BF16),
-        vmem((n3, rows, half), BF16),
+        vmem((4, ctx, rows, width // 4), BF16),
         vmem((rows, width), BF16),
         vmem((h3, rows, share), BF16),
         vmem((rows, share), BF16),
@@ -551,15 +571,14 @@
         vmem((2, width, cols), BF16),
         dma((7,)), dma((3,)),
         dma((bits, ctx)), dma((bits, ctx)),
-        dma((2, n3, nx)), dma((2, n3, nx)),
-        dma((2, n3)), dma((2, n3)),
+        dma((4, ctx)), dma((4, ctx)),
         dma((h3,)), dma((h3,)),
         dma((2,)), dma((2,)),
         dma((2, 2, n3)), dma((2, 2, n3)),
         dma((2, 2, ny * nz)), dma((2, 2, ny * nz)),
         dma((2, 2, ny * nz)), dma((2, 2, ny * nz)),
         dma((2, 2, n3)), dma((2, 2, n3)),
-        dma((2,)), dma((2,)),
+        dma((2, 2, nx)), dma((2, 2, nx)),
         pltpu.SemaphoreType.REGULAR,
     ]
     hbm = pl.BlockSpec(memory_space=pl.ANY)
@@ -581,7 +600,21 @@
         group_order, latent[0], rope_key[0].T, query_nope[0], query_rope[0],
         key_up, value_up, grad_out[0],
     )
-    return lat[None], key_grad.astype(F32), value_grad.astype(F32)
+    tall = width // 4
+    whole = pl.BlockSpec((rows, share), lambda i: (0, 0))
+    block = pl.BlockSpec((tall, cols), lambda i: (i, 0))
+    lat, key_grad, value_grad = pl.pallas_call(
+        widen,
+        grid=(width // tall,),
+        out_shape=(
+            jax.ShapeDtypeStruct((rows, share), BF16),
+            jax.ShapeDtypeStruct((width, cols), F32),
+            jax.ShapeDtypeStruct((width, cols), F32),
+        ),
+        in_specs=[whole, block, block],
+        out_specs=(whole, block, block),
+    )(lat, key_grad, value_grad)
+    return lat[None], key_grad, value_grad
 
 
 def solution(mesh):

time: 88.6 us -> 82.5 us (0.931)
  other arithmetic: 4.44 us -> 0 us
  Pallas kernels: 82.7 us -> 81.7 us
    pallas_call x1, Pallas kernels: 82.7 us -> 77.5 us  [shards(): pl.pallas_call(functools.partial(kernel, dims), out_shape=(jax.ShapeDtype...]
    convert_element_type x2 -> x0, other arithmetic: 4.44 us -> none  [shards(): return (lat[None], key_grad.astype(F32), value_grad.astype(F32))]
    pallas_call x0 -> x1, Pallas kernels: none -> 4.15 us  [shards(): pl.pallas_call(widen, grid=(width // tall,), out_shape=(jax.ShapeDtypeStr...]
where the time goes in v3:
time: 82.5 us; the launch traced here: 82.3 us
  Pallas kernels  81.7 us (99%)
    pallas_call x1, Pallas kernels, shards(): pl.pallas_call(functools.partial(kernel, dims), out_shape=(jax.ShapeDtype...  77.5 us
    pallas_call x1, Pallas kernels, shards(): pl.pallas_call(widen, grid=(width // tall,), out_shape=(jax.ShapeDtypeStr...  4.15 us

profile of v3, /device:TPU:1, one launch (start us, length us, event | category | flops | bytes accessed | tf_op | source)
XLA Modules:
  0.0 82.3 jit_solution(14235679505908497074)
XLA Ops:
  0.6 77.5 %shard_map.103 = (bf16[128,128]{1,0:T(8,128)(2,1)}, bf16[512,1024]{1,0:T(8,128)(2,1)}, bf16[512,1024]{1,0:T(8,128)(2,1)}) custom-call(s32[32]{0:T(128)} %refs_0_.1, bf16[128,512]{1,0:T(8,128)(2,1)} %bitcast.10, bf16[64,128]{1,0:T(8,128)(2,1)} %bitcast.13, bf16[128,1024]{1,0:T(8,128)(2,1)} %bitcast.8, bf16[128,512]{1,0:T(8,128)(2,1)} %bitcast.11, ...), custom_call_target="tpu_custom_call" | custom-call | flops 15000000512 | bytes 8000000 | tf_op jit(solution)/shard_map/pallas_call | solution.py:585
  78.2 4.2 %shard_map.104 = (bf16[128,128]{1,0:T(8,128)(2,1)}, f32[512,1024]{1,0:T(8,128)}, f32[512,1024]{1,0:T(8,128)}) custom-call(bf16[128,128]{1,0:T(8,128)(2,1)} %get-tuple-element.9.lat_ref, bf16[512,1024]{1,0:T(8,128)(2,1)} %get-tuple-element.10.key_ref, bf16[512,1024]{1,0:T(8,128)(2,1)} %get-tuple-element.11.value_ref), custom_call_target="tpu_custom_call" | custom-call | tf_op jit(solution)/shard_map/pallas_call | solution.py:606

commit v4 on v3

--- a/solution.py
+++ b/solution.py
@@ -13,6 +13,8 @@
 F32 = jnp.float32
 BF16 = jnp.bfloat16
 MESH = pl.DeviceIdType.MESH
+CUTS = 4
+PLAN = ("value", "v", "query", "v", "key", "k", "c0", "k", "v", "c1", "s0", "c2", "k", "v", "s1", "c3", "k", "v", "s2", "s3", "k", "v", "heads", "k", "finish", "v", "k")
 
 
 def dot_nn(left, right):
@@ -212,14 +214,17 @@
     def tile_cols(n):
         return pl.ds(mult(n, tile), tile)
 
+    cuts = [0, 4, 8, 12, 15, 16] if blocks == 16 else [0, 3, 4]
     depth = 1
-    for i in range(chunks):
-        while depth < max(j.bit_count() for j in order[4 * i:4 * i + 4]):
+    for i in range(len(cuts) - 1):
+        members = order[cuts[i]:cuts[i + 1]]
+        while depth < max(j.bit_count() for j in members):
             depth += 1
             relay(depth)
-        span = pl.ds(i * chunk, chunk)
-        for b in range(4):
-            block = block_of(order[4 * i + b])
+        height = len(members) * rows
+        span = pl.ds(cuts[i] * rows, height)
+        for b, slot in enumerate(members):
+            block = block_of(slot)
             for g in range(2):
                 k_pos = group_ref[2 * block + g] * GROUP + downs
                 bias[pl.ds(b * rows + g * GROUP, GROUP), :] = jnp.where(k_pos <= q_pos, 0.0, -jnp.inf)
@@ -227,19 +232,19 @@
             turned = dot_nt(ident, kbuf[span, pl.ds(b * 128, 128)])
             lat_t[pl.ds(b * 128, 128), span] = turned.astype(BF16)
 
-        def tile_scores(n, span=span):
+        def tile_scores(n, span=span, height=height):
             s = dot_nn(kbuf[span, :], q_t[:, n * tile:(n + 1) * tile])
-            return s + jnp.concatenate([bias[...]] * (tile // 128), axis=1)
-
-        score[:, 0:tile] = tile_scores(0)
+            return s + jnp.concatenate([bias[0:height, :]] * (tile // 128), axis=1)
+
+        score[0:height, 0:tile] = tile_scores(0)
         for n in range(tiles):
             tc = pl.ds(n * tile, tile)
             if n + 1 < tiles:
-                score[:, (n + 1) * tile:(n + 2) * tile] = tile_scores(n + 1)
+                score[0:height, (n + 1) * tile:(n + 2) * tile] = tile_scores(n + 1)
             gprob[span, tc] = dot_nn(kbuf[span, pl.ds(0, latent)], g_low[:, tc])
             old = peak[:, tc]
-            new = jnp.maximum(old, jnp.max(score[:, tc], axis=0, keepdims=True))
-            p = jnp.exp2((score[:, tc] - new) * scale)
+            new = jnp.maximum(old, jnp.max(score[0:height, tc], axis=0, keepdims=True))
+            p = jnp.exp2((score[0:height, tc] - new) * scale)
             prob[span, tc] = p.astype(BF16)
             fade = jnp.exp2((old - new) * scale)
             total[:, tc] = total[:, tc] * fade + jnp.sum(p, axis=0, keepdims=True)
@@ -249,10 +254,6 @@
             o_acc[:, tc] = o if i == 0 else o_acc[:, tc] * fade + o
         if i == 0:
             lax.fori_loop(0, heads // 2, project_rows, 0)
-        if i + 1 < chunks and depth < bits:
-            depth += 1
-            relay(depth)
-
     for z in range(1, nz):
         pl.semaphore_signal(plane, inc=1, device_id=at_z(z, 0), device_id_type=MESH)
     inv[...] = 1.0 / total[...]
@@ -265,7 +266,7 @@
         return carry
 
     lax.fori_loop(0, tiles, read_out, 0)
-    for i in range(chunks):
+    for i in range(len(cuts) - 1):
         peaks[pl.ds(i, 1), :] = jnp.exp2((peaks[pl.ds(i, 1), :] - peak[...]) * scale) * inv[...]
 
     core_rows = latent // 2
@@ -305,7 +306,7 @@
             for o in o1:
                 arrived(w1.at[w, s, o - 1], w1_s.at[w, s, o - 1], w1_r.at[w, s, o - 1], a1(o))
                 acc = acc + w1[w, s, o - 1].astype(F32)
-            w1s[w, s] = acc
+            w1s[w, s] = acc.astype(BF16)
             if w == 0 and s == 0 and nz > 1:
                 pl.semaphore_wait(plane, nz - 1)
             for o, z in pairs:
@@ -329,11 +330,11 @@
 
         for s in range(2):
             n1, i1, a1, o1, n2, i2, u2, pairs, r, rz, c = cut(s)
-            acc = w1s[w, s, pl.ds(mult(zl, rz), rz), pl.ds(mult(i2, c), c)]
+            acc = w1s[w, s, pl.ds(mult(zl, rz), rz), pl.ds(mult(i2, c), c)].astype(F32)
             for o, z in pairs:
                 slot = z * n2 + o
                 arrived(w2.at[w, s, slot], w2_s.at[w, s, slot], w2_r.at[w, s, slot], peer(o, z, u2))
-                acc = acc + w2[w, s, slot]
+                acc = acc + w2[w, s, slot].astype(F32)
             spot = place(s, i1 * r + zl * rz, mult(i2, c), rz, c)
             spot[...] = acc.astype(BF16)
             for o, z in pairs:
@@ -369,35 +370,26 @@
         own.wait()
         yield
 
-    def value_head(h, carry):
-        hc = head_cols(h)
+    def value_head(h):
+        hc = pl.ds(h * 128, 128)
         w_own[0, :, hc] = dot_nn(o_low[:, hc], go[:, hc]).astype(BF16)
-        return carry
-
-    lax.fori_loop(0, heads, value_head, 0)
-    value_chain, key_chain = chain(0), chain(1)
-    next(value_chain)
-
-    step = 128
-
-    def grade(j, carry, i=0):
-        span = pl.ds(pl.multiple_of(i * chunk + j * step, step), step)
-        p = prob[span, :].astype(F32) * peaks[pl.ds(i, 1), :]
-        prob[span, :] = p.astype(BF16)
-        dscore[span, :] = (p * (gprob[span, :] - rdot[...])).astype(BF16)
-        return carry
-
-    for i in range(chunks):
-        lax.fori_loop(0, chunk // step, functools.partial(grade, i=i), 0)
+
+    def grade(n):
+        tc = pl.ds(n * tile, tile)
+        for i in range(len(cuts) - 1):
+            for j in range(cuts[i], cuts[i + 1]):
+                span = pl.ds(j * rows, rows)
+                p = prob[span, tc].astype(F32) * peaks[pl.ds(i, 1), tc]
+                prob[span, tc] = p.astype(BF16)
+                dscore[span, tc] = (p * (gprob[span, tc] - rdot[:, tc])).astype(BF16)
 
     def query_grad(n):
         tc = pl.ds(n * tile, tile)
         gq_low[:, tc] = (dot_nn(lat_t[...], dscore[:, tc]) * factor).astype(BF16)
 
-    def key_head(h, carry):
-        hc = head_cols(h)
+    def key_head(h):
+        hc = pl.ds(h * 128, 128)
         w_own[1, :, hc] = dot_nn(gq_low[:, hc], qn[:, hc]).astype(BF16)
-        return carry
 
     if bits == 4:
         stages = (((0,), (1,), (2, 3)), ((2,), (3,), (0, 1)), ((1,), (0,), (2, 3)), ((3,), (2,), (0, 1)))
@@ -451,62 +443,74 @@
         for _, _, k, j in sorted(todo):
             latent_send(k, j)
 
-    for n in range(tiles):
-        query_grad(n)
-    next(value_chain)
-    lax.fori_loop(0, heads, key_head, 0)
-    next(key_chain)
-    latent_chunk(0)
-    next(key_chain)
-    latent_sends(0)
-    if chunks > 1:
-        latent_chunk(1)
-        next(value_chain)
-        latent_sends(1)
-        latent_chunk(2)
-        latent_sends(2)
-        next(key_chain)
-        latent_chunk(3)
-        next(value_chain)
-        latent_sends(3)
-    else:
-        next(value_chain)
-        next(key_chain)
-        next(value_chain)
-    next(key_chain)
-    next(value_chain)
-    next(key_chain)
-    for k in range(4):
-        lzs[:, pl.ds(k * width, width)] = latent_sum(k, 0).astype(BF16)
     share = latent // nh
-    for o in range(1, nh):
-        send(
-            lzs.at[:, pl.ds(mult(lax.rem(head + o, nh), share), share)], lzr.at[o - 1],
-            lz_s.at[o - 1], lz_r.at[o - 1], at_head(o),
-        )
-    next(value_chain)
-    next(key_chain)
-    acc = lzs[:, pl.ds(mult(head, share), share)].astype(F32)
-    for o in range(1, nh):
-        arrived(lzr.at[o - 1], lz_s.at[o - 1], lz_r.at[o - 1], at_head(o))
-        acc = acc + lzr[o - 1].astype(F32)
-    lat_v[...] = acc.astype(BF16)
-    out = pltpu.make_async_copy(lat_v, lat_out, out_sem.at[2])
-    out.start()
-    live = [value_chain, key_chain]
-    while live:
-        for c in list(live):
-            if next(c, "end") == "end":
-                live.remove(c)
-    out.wait()
+    chains = {"v": chain(0), "k": chain(1)}
+
+    def latent_heads():
+        for k in range(4):
+            lzs[:, pl.ds(k * width, width)] = latent_sum(k, 0).astype(BF16)
+        for o in range(1, nh):
+            send(
+                lzs.at[:, pl.ds(mult(lax.rem(head + o, nh), share), share)], lzr.at[o - 1],
+                lz_s.at[o - 1], lz_r.at[o - 1], at_head(o),
+            )
+
+    def latent_finish():
+        acc = lzs[:, pl.ds(mult(head, share), share)].astype(F32)
+        for o in range(1, nh):
+            arrived(lzr.at[o - 1], lz_s.at[o - 1], lz_r.at[o - 1], at_head(o))
+            acc = acc + lzr[o - 1].astype(F32)
+        lat_v[...] = acc.astype(BF16)
+        last = pltpu.make_async_copy(lat_v, lat_out, out_sem.at[2])
+        last.start()
+        last.wait()
+
+    for op in PLAN:
+        if op in chains:
+            next(chains[op])
+        elif op == "value":
+            for h in range(heads):
+                value_head(h)
+        elif op == "query":
+            for n in range(tiles):
+                grade(n)
+                query_grad(n)
+        elif op == "key":
+            for h in range(heads):
+                key_head(h)
+        elif op == "heads":
+            latent_heads()
+        elif op == "finish":
+            latent_finish()
+        elif int(op[1]) < chunks:
+            (latent_chunk if op[0] == "c" else latent_sends)(int(op[1]))
     for copy in sends:
         copy.wait_send()
 
 
-def widen(lat_ref, key_ref, value_ref, lat_out, key_out, value_out):
-    lat_out[...] = lat_ref[...]
-    key_out[...] = key_ref[...].astype(F32)
-    value_out[...] = value_ref[...].astype(F32)
+def widen(lat_ref, key_ref, value_ref, lat_out, key_out, value_out, lat_v, low, wide, in_sem, out_sem):
+    tall = low.shape[1] // CUTS
+    pairs = ((key_ref, key_out), (value_ref, value_out))
+    loads, stores = [], []
+    for c in range(CUTS):
+        for a, (src, _) in enumerate(pairs):
+            span = pl.ds(c * tall, tall)
+            loads.append(pltpu.make_async_copy(src.at[span], low.at[a, span], in_sem.at[a, c]))
+            loads[-1].start()
+    lat = pltpu.make_async_copy(lat_ref, lat_v, in_sem.at[2, 0])
+    lat.start()
+    for c in range(CUTS):
+        for a, (_, dst) in enumerate(pairs):
+            span = pl.ds(c * tall, tall)
+            loads[2 * c + a].wait()
+            wide[a, span, :] = low[a, span, :].astype(F32)
+            stores.append(pltpu.make_async_copy(wide.at[a, span], dst.at[span], out_sem.at[a, c]))
+            stores[-1].start()
+    lat.wait()
+    stores.append(pltpu.make_async_copy(lat_v, lat_out, out_sem.at[2, 0]))
+    stores[-1].start()
+    for copy in stores:
+        copy.wait()
 
 
 def shards(query_nope, query_rope, latent, rope_key, key_up, value_up, grad_out, group_order):
@@ -566,8 +570,8 @@
         vmem((2, width // 2, cols), BF16),
         vmem((2, width // 2, cols), BF16),
         vmem((2, 2, n3, r1, cols), BF16),
-        vmem((2, 2, r1, cols), F32),
-        vmem((2, 2, ny * nz, r1 // nz, cols // ny), F32),
+        vmem((2, 2, r1, cols), BF16),
+        vmem((2, 2, ny * nz, r1 // nz, cols // ny), BF16),
         vmem((2, width, cols), BF16),
         dma((7,)), dma((3,)),
         dma((bits, ctx)), dma((bits, ctx)),
@@ -600,19 +604,20 @@
         group_order, latent[0], rope_key[0].T, query_nope[0], query_rope[0],
         key_up, value_up, grad_out[0],
     )
-    tall = width // 4
-    whole = pl.BlockSpec((rows, share), lambda i: (0, 0))
-    block = pl.BlockSpec((tall, cols), lambda i: (i, 0))
     lat, key_grad, value_grad = pl.pallas_call(
         widen,
-        grid=(width // tall,),
         out_shape=(
             jax.ShapeDtypeStruct((rows, share), BF16),
             jax.ShapeDtypeStruct((width, cols), F32),
             jax.ShapeDtypeStruct((width, cols), F32),
         ),
-        in_specs=[whole, block, block],
-        out_specs=(whole, block, block),
+        in_specs=[hbm] * 3,
+        out_specs=(hbm,) * 3,
+        scratch_shapes=[
+            vmem((rows, share), BF16), vmem((2, width, cols), BF16), vmem((2, width, cols), F32),
+            dma((3, CUTS)), dma((3, CUTS)),
+        ],
+        compiler_params=pltpu.CompilerParams(vmem_limit_bytes=60 * 1024 * 1024),
     )(lat, key_grad, value_grad)
     return lat[None], key_grad, value_grad
 

time: 82.5 us -> 75.9 us (0.920)
  Pallas kernels: 81.7 us -> 75 us
    pallas_call x1, Pallas kernels: 77.5 us -> 71.8 us  [shards(): pl.pallas_call(functools.partial(kernel, dims), out_shape=(jax.ShapeDtype...]
    pallas_call x1, Pallas kernels: 4.15 us -> 3.2 us  [shards(): pl.pallas_call(widen, out_shape=(jax.ShapeDtypeStruct((rows, share), BF16...]
where the time goes in v4:
time: 75.9 us; the launch traced here: 75.8 us
  Pallas kernels  75 us (99%)
  between operations  0.8 us (1%)
    pallas_call x1, Pallas kernels, shards(): pl.pallas_call(functools.partial(kernel, dims), out_shape=(jax.ShapeDtype...  71.8 us
    pallas_call x1, Pallas kernels, shards(): pl.pallas_call(widen, out_shape=(jax.ShapeDtypeStruct((rows, share), BF16...  3.2 us

profile of v4, /device:TPU:1, one launch (start us, length us, event | category | flops | bytes accessed | tf_op | source)
XLA Modules:
  0.0 75.8 jit_solution(4953157974542276113)
XLA Ops:
  0.6 71.8 %shard_map.103 = (bf16[128,128]{1,0:T(8,128)(2,1)}, bf16[512,1024]{1,0:T(8,128)(2,1)}, bf16[512,1024]{1,0:T(8,128)(2,1)}) custom-call(s32[32]{0:T(128)} %refs_0_.1, bf16[128,512]{1,0:T(8,128)(2,1)} %bitcast.10, bf16[64,128]{1,0:T(8,128)(2,1)} %bitcast.13, bf16[128,1024]{1,0:T(8,128)(2,1)} %bitcast.8, bf16[128,512]{1,0:T(8,128)(2,1)} %bitcast.11, ...), custom_call_target="tpu_custom_call" | custom-call | flops 15000000512 | bytes 8000000 | tf_op jit(solution)/shard_map/pallas_call | solution.py:589
  72.4 3.2 %shard_map.104 = (bf16[128,128]{1,0:T(8,128)(2,1)}, f32[512,1024]{1,0:T(8,128)}, f32[512,1024]{1,0:T(8,128)}) custom-call(bf16[128,128]{1,0:T(8,128)(2,1)} %get-tuple-element.9.lat_ref, bf16[512,1024]{1,0:T(8,128)(2,1)} %get-tuple-element.10.key_ref, bf16[512,1024]{1,0:T(8,128)(2,1)} %get-tuple-element.11.value_ref), custom_call_target="tpu_custom_call" | custom-call | tf_op jit(solution)/shard_map/pallas_call | solution.py:607

commit v5 on v4

--- a/solution.py
+++ b/solution.py
@@ -14,7 +14,7 @@
 BF16 = jnp.bfloat16
 MESH = pl.DeviceIdType.MESH
 CUTS = 4
-PLAN = ("value", "v", "query", "v", "key", "k", "c0", "k", "v", "c1", "s0", "c2", "k", "v", "s1", "c3", "k", "v", "s2", "s3", "k", "v", "heads", "k", "finish", "v", "k")
+PLAN = ("value", "v", "query", "v", "key", "k", "c0", "k", "v", "c1", "s0", "c2", "k", "v", "s1", "c3", "s2", "k", "v", "s3", "k", "v", "heads", "k", "finish", "v", "k")
 
 
 def dot_nn(left, right):
@@ -95,8 +95,8 @@
     def at_head(off):
         return {"head": lax.rem(head + off, nh)}
 
-    x_offs = list(range(1, nx))
-    y_offs = list(range(1, ny))
+    x_offs = sorted(range(1, nx), key=lambda o: -o.bit_count())
+    y_offs = sorted(range(1, ny), key=lambda o: -o.bit_count())
     partners = (
         [at_slot(1 << t) for t in range(bits)] + [at_core()]
         + [at_z(z, 0) for z in range(1, nz)] + [at_head(o) for o in range(1, nh)]
@@ -279,6 +279,7 @@
         def cut(s):
             (n1, i1, a1, o1, u1), (n2, i2, a2, o2, u2) = first[s], first[1 - s]
             pairs = [(o, z) for z in range(nz) for o in range(n2) if o or z]
+            pairs.sort(key=lambda p: -p[0].bit_count() - p[1])
             return n1, i1, a1, o1, n2, i2, u2, pairs, hw // n1, hw // n1 // nz, cols // n2
 
         def peer(o, z, u2):

time: 75.9 us -> 75.1 us (0.989)
  Pallas kernels: 75 us -> 74.2 us
    pallas_call x1, Pallas kernels: 71.8 us -> 71 us  [shards(): pl.pallas_call(functools.partial(kernel, dims), out_shape=(jax.ShapeDtype...]
where the time goes in v5:
time: 75.1 us; the launch traced here: 75 us
  Pallas kernels  74.2 us (99%)
  between operations  0.8 us (1%)
    pallas_call x1, Pallas kernels, shards(): pl.pallas_call(functools.partial(kernel, dims), out_shape=(jax.ShapeDtype...  71 us
    pallas_call x1, Pallas kernels, shards(): pl.pallas_call(widen, out_shape=(jax.ShapeDtypeStruct((rows, share), BF16...  3.2 us

profile of v5, /device:TPU:1, one launch (start us, length us, event | category | flops | bytes accessed | tf_op | source)
XLA Modules:
  0.0 75.0 jit_solution(16484897192178184795)
XLA Ops:
  0.6 71.0 %shard_map.103 = (bf16[128,128]{1,0:T(8,128)(2,1)}, bf16[512,1024]{1,0:T(8,128)(2,1)}, bf16[512,1024]{1,0:T(8,128)(2,1)}) custom-call(s32[32]{0:T(128)} %refs_0_.1, bf16[128,512]{1,0:T(8,128)(2,1)} %bitcast.10, bf16[64,128]{1,0:T(8,128)(2,1)} %bitcast.13, bf16[128,1024]{1,0:T(8,128)(2,1)} %bitcast.8, bf16[128,512]{1,0:T(8,128)(2,1)} %bitcast.11, ...), custom_call_target="tpu_custom_call" | custom-call | flops 15000000512 | bytes 8000000 | tf_op jit(solution)/shard_map/pallas_call | solution.py:590
  71.6 3.2 %shard_map.104 = (bf16[128,128]{1,0:T(8,128)(2,1)}, f32[512,1024]{1,0:T(8,128)}, f32[512,1024]{1,0:T(8,128)}) custom-call(bf16[128,128]{1,0:T(8,128)(2,1)} %get-tuple-element.9.lat_ref, bf16[512,1024]{1,0:T(8,128)(2,1)} %get-tuple-element.10.key_ref, bf16[512,1024]{1,0:T(8,128)(2,1)} %get-tuple-element.11.value_ref), custom_call_target="tpu_custom_call" | custom-call | tf_op jit(solution)/shard_map/pallas_call | solution.py:608
